TPU v7x, 256 devices: a whole 4x4x8 slice. The times are simulated.
256 devices in a mesh: band: 4 (over y), dx: 8 (over z), dy: 8 (over x, core).
Axes of the slice: x: 4, y: 4, z: 8, core: 2. Of those that a mesh axis runs over, the one named last changes fastest.
Arguments:
- wave_bands: float32 [4, 64, 128, 128], P('band', 'dx', 'dy'), may hold values from -6 to 6
- potential: float32 [64, 128, 128], P('dx', 'dy', 'band'), may hold values from -1.5 to 0.5
- atom_offsets: int32 [8, 8, 4, 3], P('dx', 'dy'), may hold values from 0 to 95, as said below
- proj_counts: int32 [8, 8, 4], P('dx', 'dy'), may hold values from 0 to 9, as said below
- dh_matrix: float32 [8, 8, 4, 9, 9], P('dx', 'dy'), as said below
- ds_matrix: float32 [8, 8, 4, 9, 9], P('dx', 'dy'), as said below
Outputs:
- new_bands: float32 [4, 64, 128, 128], P('band', 'dx', 'dy')
- new_residual: float32 [4, 64, 128, 128], P('band', 'dx', 'dy')
- band_energy: float32 [4], P('band')
Inputs may be any that keep to these rules, and one draw needn't show every extreme that they name: `atom_offsets`: columns are x in 0..7, y in 0..15, z in 32..3*128/4-1. `proj_counts`: each count is 0 (empty slot), 1, 4 or 9. `dh_matrix`: each matrix is symmetric. `ds_matrix`: each matrix is symmetric, and each diagonal entry exceeds the sum of the magnitudes of the other entries in its row.
All inputs are finite; a program needn't handle non-finite values.
Results may differ from a plain program's by a relative error of at most 0.00017.
Values sent between devices are 32-bit elements; how exact they have to be, the bound alone decides.
A program may use at most 64 MiB of HBM per device.

v0:
```python
import functools

import jax
import jax.numpy as jnp
import numpy as np
from jax import lax
from jax.experimental import pallas as pl
from jax.experimental.pallas import tpu as pltpu
from jax.sharding import PartitionSpec as P

MESH = pl.DeviceIdType.MESH
HIGHEST = lax.Precision.HIGHEST
F32 = jnp.float32

STENCIL = (-49.0 / 18.0, 1.5, -0.15, 1.0 / 90.0)
RELAXATION = 2.0 / 3.0
MASS_SHIFT = 0.25
AMPLITUDE = 0.15
D_NORM = 0.28867513
CX, CY, NZ = 8, 16, 128
ATOMS = 4

DIAG = [3.0 / 4.0**level + MASS_SHIFT for level in range(3)]
GAIN = [RELAXATION / d for d in DIAG]
SIDE = [0.5 * GAIN[level] / 4.0**level for level in range(3)]


def pad8(n):
    return (n + 7) // 8 * 8


def cells(x0, x1, y0, y1):
    return [(i, j) for i in range(x0, x1) for j in range(y0, y1)]


def cross(out, inp):
    where = {c: n for n, c in enumerate(inp)}
    m = np.zeros((len(out), len(inp)))
    for row, (i, j) in enumerate(out):
        for c in ((i - 1, j), (i + 1, j), (i, j - 1), (i, j + 1)):
            if c in where:
                m[row, where[c]] = 1.0
    return m


def pick(out, inp):
    where = {c: n for n, c in enumerate(inp)}
    m = np.zeros((len(out), len(inp)))
    for row, c in enumerate(out):
        if c in where:
            m[row, where[c]] = 1.0
    return m


def average(out, inp):
    where = {c: n for n, c in enumerate(inp)}
    m = np.zeros((len(out), len(inp)))
    for row, (i, j) in enumerate(out):
        for c in cells(2 * i, 2 * i + 2, 2 * j, 2 * j + 2):
            if c in where:
                m[row, where[c]] = 0.25
    return m


def spread_to(out, inp):
    where = {c: n for n, c in enumerate(inp)}
    m = np.zeros((len(out), len(inp)))
    for row, (i, j) in enumerate(out):
        m[row, where[(i // 2, j // 2)]] = 1.0
    return m


def along_z(n):
    return np.eye(n, k=1) + np.eye(n, k=-1)


def halve_z(n):
    return np.repeat(np.eye(n // 2), 2, axis=0) * 0.5


def double_z(n):
    return np.repeat(np.eye(n), 2, axis=1)


def both(m):
    z = np.zeros_like(m)
    return np.block([[m, z], [z, m]])


def grown(m, rows, cols):
    out = np.zeros((rows, cols))
    out[: m.shape[0], : m.shape[1]] = m
    return out


FINE = cells(0, CX, 0, CY)
ONE = cells(-1, 5, -1, 9)
ONE_WIDE = cells(-2, 6, -2, 10)
TWO = cells(-1, 3, -1, 5)
TWO_WIDE = cells(-3, 5, -3, 7)

NEAR = [(a, b) for a in (-1, 0, 1) for b in (-1, 0, 1) if (a, b) != (0, 0)]
FAR = [(a, b) for a in (-2, -1, 0, 1, 2) for b in (-1, 0, 1) if (a, b) != (0, 0)]
RING = [(a, b) for a in range(-2, 3) for b in range(-2, 3) if (a, b) != (0, 0)]


def blocks(own, wide, step, targets):
    wide = set(wide)
    table, at = {}, 0
    for t in targets:
        block = [c for c in own if (c[0] - step[0] * t[0], c[1] - step[1] * t[1]) in wide]
        table[t] = (at, block)
        at += pad8(len(block))
    return table, at


BLOCKS_ONE, ROWS_ONE = blocks(ONE, ONE_WIDE, (4, 8), NEAR)
BLOCKS_TWO, ROWS_TWO = blocks(TWO, TWO_WIDE, (2, 4), FAR)
OWN_ONE = pad8(len(ONE))
OWN_TWO = pad8(len(TWO))
STACK_ONE = ROWS_ONE + OWN_ONE
STACK_TWO = ROWS_TWO + OWN_TWO


def senders(table, rows, own):
    m = np.zeros((rows + pad8(len(own)), len(own)))
    for at, block in table.values():
        m[at : at + len(block)] = pick(block, own)
    m[rows : rows + len(own)] = np.eye(len(own))
    return m


def receivers(table, rows, own, wide, step):
    m = np.zeros((len(wide), rows + pad8(len(own))))
    for t, (at, block) in table.items():
        here = [(i - step[0] * t[0], j - step[1] * t[1]) for i, j in block]
        m[:, at : at + len(block)] = pick(wide, here)
    m[:, rows : rows + len(own)] = pick(wide, own)
    return m


def constants():
    c = {}
    stack = {}
    kin_own = np.zeros((128, 128))
    kin_side = np.zeros((128, 144))
    kin_z = np.zeros((NZ, NZ))
    halo = (
        cells(-3, 0, 0, CY)
        + cells(8, 11, 0, CY)
        + [(x, y) for y in range(-3, 0) for x in range(CX)]
        + [(x, y) for y in range(16, 19) for x in range(CX)]
    )
    where_own = {cell: n for n, cell in enumerate(FINE)}
    where_halo = {cell: n for n, cell in enumerate(halo)}
    for row, (x, y) in enumerate(FINE):
        kin_own[row, row] = -1.5 * STENCIL[0]
        for reach in (1, 2, 3):
            for cell in ((x - reach, y), (x + reach, y), (x, y - reach), (x, y + reach)):
                if cell in where_own:
                    kin_own[row, where_own[cell]] += -0.5 * STENCIL[reach]
                else:
                    kin_side[row, where_halo[cell]] += -0.5 * STENCIL[reach]
    for reach in (1, 2, 3):
        kin_z += -0.5 * STENCIL[reach] * (np.eye(NZ, k=reach) + np.eye(NZ, k=-reach))
    c["kin_own"], c["kin_side"], c["kin_z"] = kin_own, kin_side, kin_z

    ring0 = cells(-2, 10, -2, 18)
    avg = average(ONE, ring0)
    one_plane = avg @ (pick(ring0, FINE) / 3.0 + SIDE[0] * cross(ring0, FINE))
    one_along = avg @ pick(ring0, FINE) * SIDE[0]
    send = senders(BLOCKS_ONE, ROWS_ONE, ONE)
    c["down_one"] = np.concatenate([send @ one_plane, send @ one_along], axis=1)
    half = halve_z(NZ)
    c["down_one_z"] = np.concatenate([both(half), both(along_z(NZ) @ half)], axis=1)

    ring1 = cells(-2, 6, -2, 10)
    avg = average(TWO, ring1)
    two_plane = avg @ (pick(ring1, ONE) / 3.0 + SIDE[1] * cross(ring1, ONE))
    two_along = avg @ pick(ring1, ONE) * SIDE[1]
    send = senders(BLOCKS_TWO, ROWS_TWO, TWO)
    c["down_two"] = np.concatenate(
        [grown(send @ two_plane, STACK_TWO, OWN_ONE), grown(send @ two_along, STACK_TWO, OWN_ONE)], axis=1
    )
    half = halve_z(64)
    c["down_two_z"] = np.concatenate(
        [grown(both(half), 128, 128), grown(both(along_z(64) @ half), 128, 128)], axis=1
    )

    take = receivers(BLOCKS_TWO, ROWS_TWO, TWO, TWO_WIDE, (2, 4))
    mid = cells(-2, 4, -2, 6)
    n1 = cross(TWO, TWO_WIDE)
    n2 = cross(TWO, mid) @ cross(mid, TWO_WIDE)
    here = pick(TWO, TWO_WIDE)
    g, k = GAIN[2], SIDE[2]
    terms = [
        g * (13.0 / 9.0 * here + 5.0 / 3.0 * k * n1 + k * k * n2),
        g * (5.0 / 3.0 * k * here + 2.0 * k * k * n1),
        g * k * k * here,
    ]
    c["sweep_two"] = np.concatenate([t @ take for t in terms], axis=1)
    nz = along_z(32)
    c["sweep_two_z"] = np.concatenate(
        [grown(both(m), 128, 128) for m in (np.eye(32), nz, nz @ nz)], axis=1
    )

    take = receivers(BLOCKS_ONE, ROWS_ONE, ONE, ONE_WIDE, (4, 8))
    g, k = GAIN[1], SIDE[1]
    here, n1 = pick(ONE, ONE_WIDE), cross(ONE, ONE_WIDE)
    up = spread_to(ONE_WIDE, TWO)
    c["up_one"] = grown(
        np.concatenate(
            [
                g * (4.0 / 3.0 * here + k * n1) @ take,
                g * k * here @ take,
                (here / 3.0 + k * n1) @ up,
                k * here @ up,
            ],
            axis=1,
        ),
        OWN_ONE,
        2 * STACK_ONE + 2 * len(TWO),
    )
    nz = along_z(64)
    c["one_z"] = both(nz)
    double = double_z(32)
    c["up_one_z"] = np.concatenate(
        [grown(both(double), 128, 128), grown(both(double @ nz), 128, 128)], axis=1
    )

    g, k = GAIN[0], SIDE[0]
    ring0 = cells(-1, 9, -1, 17)
    here, n1 = pick(FINE, ring0), cross(FINE, ring0)
    up = spread_to(ring0, ONE)
    faces = (
        cells(-1, 0, 0, CY) + cells(8, 9, 0, CY) + [(x, -1) for x in range(CX)] + [(x, 16) for x in range(CX)]
    )
    c["up_zero"] = np.concatenate(
        [
            g * (4.0 / 3.0 * np.eye(128) + k * cross(FINE, FINE)),
            grown((here / 3.0 + k * n1) @ up, 128, OWN_ONE),
            grown(k * here @ up, 128, OWN_ONE),
            g * k * cross(FINE, faces),
        ],
        axis=1,
    )
    nz = along_z(NZ)
    double = double_z(64)
    c["zero_z"] = g * k * nz
    c["up_zero_z"] = np.concatenate([grown(double, 128, 128), grown(double @ nz, 128, 128)], axis=1)
    return {name: m.astype(np.float32) for name, m in c.items()}


NAMES = (
    "kin_own",
    "kin_side",
    "kin_z",
    "down_one",
    "down_one_z",
    "down_two",
    "down_two_z",
    "sweep_two",
    "sweep_two_z",
    "up_one",
    "one_z",
    "up_one_z",
    "up_zero",
    "zero_z",
    "up_zero_z",
)


def mm(a, b):
    return lax.dot_general(a, b, (((1,), (0,)), ((), ())), precision=HIGHEST, preferred_element_type=F32)


def mm_t(a, b):
    return lax.dot_general(a, b, (((1,), (1,)), ((), ())), precision=HIGHEST, preferred_element_type=F32)


def projector_of(p, right):
    left_of = jnp.where(p < 3, p, jnp.where(p == 3, 4, jnp.where(p == 4, 7, 99)))
    right_of = jnp.where(p == 0, 3, jnp.where(p < 3, p + 4, jnp.where(p < 5, 8, 99)))
    return jnp.where(right, right_of, left_of)


def kernel(shape, *refs):
    nb, nx, ny = shape
    w_ref, pot_ref, offs_ref, cnt_ref, dh_ref, ds_ref = refs[:6]
    const = dict(zip(NAMES, refs[6 : 6 + len(NAMES)]))
    outs = refs[6 + len(NAMES) : 9 + len(NAMES)]
    bands_ref, resid_ref, energy_ref = outs
    (
        stage, halo, halo2, dirs, info, infos, infot, pots, qbuf, qrecv, qbuf2, qrecv2,
        fields, bface, bhalo, one_s, one_r, two_s, two_r, esend, ebuf, lsend, lbuf, zfun, wfun,
        ssem, rsem,
    ) = refs[9 + len(NAMES) :]
    ib, ix, iy = lax.axis_index("band"), lax.axis_index("dx"), lax.axis_index("dy")

    def device(a, b, band=0):
        return (lax.rem(ib + band + nb, nb), lax.rem(ix + a + nx, nx), lax.rem(iy + b + ny, ny))

    def send(src, dst, k, where):
        pltpu.make_async_remote_copy(
            src_ref=src, dst_ref=dst, send_sem=ssem.at[k], recv_sem=rsem.at[k], device_id=where, device_id_type=MESH
        ).start()

    def arrive(ref, k):
        pltpu.make_async_copy(ref, ref, rsem.at[k]).wait()

    def left(ref, k):
        pltpu.make_async_copy(ref, ref, ssem.at[k]).wait()

    me = ix * ny + iy
    slot = lax.rem(ix, 4) * 4 + lax.rem(iy, 4)

    infos[...] = jnp.zeros_like(infos)
    barrier = pltpu.get_barrier_semaphore()

    def greet(i, carry):
        a, b = i // ny, lax.rem(i, ny)
        pl.semaphore_signal(barrier, inc=1, device_id=device(a, b), device_id_type=MESH)
        return carry

    lax.fori_loop(1, nx * ny, greet, 0)
    for i in range(1, nb):
        pl.semaphore_signal(barrier, inc=1, device_id=device(0, 0, i), device_id_type=MESH)

    for j in range(3):
        stage[8 * j : 8 * j + 8, :] = w_ref[pl.ds(j, 8, stride=16), :]
        stage[24 + 8 * j : 32 + 8 * j, :] = w_ref[pl.ds(13 + j, 8, stride=16), :]
    row = lax.broadcasted_iota(jnp.int32, (128, 128), 0)
    lane = lax.broadcasted_iota(jnp.int32, (1, 128), 1)
    place = (lax.broadcasted_iota(jnp.int32, (32, 128), 0) + 32 * ib == lax.broadcasted_iota(jnp.int32, (32, 128), 1)).astype(F32)
    pots[ib] = mm(pot_ref[...], place)
    crossed, p_from, p_to = lane // 40, (lane // 8) % 5, lane % 8
    which = lax.broadcasted_iota(jnp.int32, (9, 128), 0)
    lane4 = lax.broadcasted_iota(jnp.int32, (ATOMS, 128), 1)
    atom4 = lax.broadcasted_iota(jnp.int32, (ATOMS, 128), 0)
    for right in (0, 1):
        j_of = projector_of(p_from, (crossed != right))
        i_of = projector_of(p_to, lane * 0 + right == 1)
        chosen = ((which == i_of) & (lane < 80)).astype(F32)
        place_of = jnp.zeros((ATOMS, 128), F32)
        for k in range(ATOMS):
            for m, v in enumerate((offs_ref[0, 0, k, 0], offs_ref[0, 0, k, 1], offs_ref[0, 0, k, 2], cnt_ref[0, 0, k])):
                place_of = jnp.where((atom4 == k) & (lane4 == 80 + m), v.astype(F32), place_of)
        for n, ref in enumerate((dh_ref, ds_ref)):
            full = jnp.zeros((ATOMS, 9, 128), F32)
            for j in range(9):
                full = full + ref[:, :, j : j + 1] * (j_of == j).astype(F32)[None]
            rows = jnp.sum(full * chosen[None], axis=1)
            info[4 * right : 4 * right + 4, 128 * n : 128 * n + 128] = rows + place_of if n == 0 else rows
    infos[slot] = info[...]

    pl.semaphore_wait(barrier, nx * ny - 1 + nb - 1)

    for a, b in NEAR:
        send(info, infos.at[slot], 0, device(a, b))
    send(w_ref.at[pl.ds(0, 48)], halo.at[pl.ds(48, 48)], 1, device(-1, 0))
    send(w_ref.at[pl.ds(80, 48)], halo.at[pl.ds(0, 48)], 1, device(1, 0))
    send(stage.at[pl.ds(0, 24)], halo.at[pl.ds(120, 24)], 1, device(0, -1))
    send(stage.at[pl.ds(24, 24)], halo.at[pl.ds(96, 24)], 1, device(0, 1))
    for i in range(1, nb):
        send(pots.at[ib], pots.at[ib], 2, device(0, 0, i))
    w = w_ref[...]
    kin = mm(const["kin_own"][...], w) + mm(w, const["kin_z"][...])

    arrive(infos.at[pl.ds(0, 8)], 0)
    for n in range(2):
        infot[n] = jnp.swapaxes(infos[:, :, 128 * n : 128 * n + 128].reshape(128, 128), 0, 1)
    slot_x, slot_y = lane // 32, (lane // 8) % 4
    right_lane = (lane // 4) % 2 == 1
    rel_x = lax.rem(slot_x - ix + 1 + 16, 4) - 1
    rel_y = lax.rem(slot_y - iy + 1 + 16, 4) - 1
    own_lane = ((rel_x == 0) & (rel_y == 0)).astype(F32)
    centre_x = infot[0, 80:81, :] + (rel_x * CX).astype(F32)
    centre_y = infot[0, 81:82, :] + (rel_y * CY).astype(F32)
    centre_z = infot[0, 82:83, :]
    count = infot[0, 83:84, :]
    row8 = lax.broadcasted_iota(jnp.int32, (8, 128), 0)
    active = (projector_of(row8, jnp.broadcast_to(right_lane, (8, 128))).astype(F32) < count).astype(F32)

    def bells(n, centre):
        r = lax.broadcasted_iota(jnp.int32, (n, 128), 0).astype(F32) - centre
        inside = ((r > -6.5) & (r < 5.5)).astype(F32)
        q = r * r
        return r, q, [inside * jnp.exp(q * (-1.0 / s)) for s in (8.0, 9.68, 11.52)]

    rz, qz, (zs, zp, zd) = bells(NZ, centre_z)
    zp, zd = zp * (1.0 / 2.2), zd * (1.0 / 5.76)
    zfun[0] = jnp.where(right_lane, rz * zp, zs)
    zfun[1] = jnp.where(right_lane, rz * zd, zp)
    zfun[2] = jnp.where(right_lane, qz * zd, zd)
    zfun[3] = zd
    rx, qx, (xs, xp, xd) = bells(CX, centre_x)
    ry, qy, (ys, yp, yd) = bells(CY, centre_y)
    pairs = (
        (jnp.where(right_lane, xp, xs), jnp.where(right_lane, yp, ys)),
        (jnp.where(right_lane, xd, rx * xp), jnp.where(right_lane, ry * yd, yp)),
        (jnp.where(right_lane, rx * xd, xp), jnp.where(right_lane, yd, ry * yp)),
        (jnp.where(right_lane, xd, rx * xd), jnp.where(right_lane, (2.0 * D_NORM) * yd, ry * yd)),
    )
    for p, (fx, fy) in enumerate(pairs):
        wfun[p] = ((AMPLITUDE * fx)[:, None, :] * fy[None, :, :]).reshape(128, 128)
    on_x = jnp.where(right_lane, -D_NORM, 0.5) * AMPLITUDE
    on_y = jnp.where(right_lane, -D_NORM, -0.5) * AMPLITUDE
    wfun[4] = (
        (on_x * qx * xd)[:, None, :] * yd[None, :, :] + xd[:, None, :] * (on_y * qy * yd)[None, :, :]
    ).reshape(128, 128)
    tile_of = (0, 1, 1, 2, 3)

    def overlaps(field):
        part = [mm(field, zfun[t]) for t in range(4)]
        rows = [jnp.sum(part[tile_of[p]] * wfun[p], axis=0, keepdims=True) for p in range(5)]
        return jnp.concatenate(rows + [jnp.zeros((3, 128), F32)], axis=0)

    keep_x = {-2: (rel_x == -1).astype(F32), 2: (rel_x == 1).astype(F32)}
    keep_y = {-2: (rel_y == -1).astype(F32), 2: (rel_y == 1).astype(F32)}

    def gather_overlaps(own, ref):
        total = None
        for a in range(-2, 3):
            line = None
            for b in range(-2, 3):
                v = own if (a, b) == (0, 0) else ref[RING.index((a, b))]
                v = v * keep_y[b] if b in keep_y else v
                line = v if line is None else line + v
            line = line * keep_x[a] if a in keep_x else line
            total = line if total is None else total + line
        return total * active

    def coefficients(q, n):
        swapped = jnp.where(right_lane, pltpu.roll(q, 4, 1), pltpu.roll(q, 124, 1))
        total = None
        for c, v in enumerate((q, swapped)):
            for p in range(5):
                at = (c * 5 + p) * 8
                term = infot[n, at : at + 8, :] * v[p : p + 1, :]
                total = term if total is None else total + term
        return total * active

    def correction(coefs):
        total = None
        for t in range(4):
            weight = None
            for p in range(5):
                if tile_of[p] == t:
                    term = wfun[p] * coefs[p : p + 1, :]
                    weight = term if weight is None else weight + term
            term = mm_t(weight, zfun[t])
            total = term if total is None else total + term
        return total

    def ring_send(src, dst, k):
        for a, b in RING:
            send(src, dst.at[RING.index((-a, -b))], k, device(a, b))

    q_own = overlaps(w)
    qbuf[...] = q_own
    ring_send(qbuf, qrecv, 3)

    arrive(halo, 1)
    kin = kin + mm(const["kin_side"][...], halo[...])
    if nb > 1:
        arrive(pots.at[pl.ds(0, nb - 1)], 2)
    potential = pots[0]
    for i in range(1, nb):
        potential = potential + pots[i]
    h_local = kin + potential * w
    num_local = jnp.sum(w * h_local, axis=0, keepdims=True)
    den_local = jnp.sum(w * w, axis=0, keepdims=True)

    arrive(qrecv, 3)
    q = gather_overlaps(q_own, qrecv)
    coef_h, coef_s = coefficients(q, 0), coefficients(q, 1)

    def total_of(v):
        return jnp.sum(v, axis=1, keepdims=True)

    num = total_of(num_local + jnp.sum(q * coef_h, axis=0, keepdims=True) * own_lane)
    den = total_of(den_local + jnp.sum(q * coef_s, axis=0, keepdims=True) * own_lane)

    def share(first, second, mine, table, k):
        mine[...] = jnp.where(lane < 64, first, second)
        table[me] = mine[...]

        def one(i, carry):
            send(mine, table.at[me], k, device(i // ny, lax.rem(i, ny)))
            return carry

        lax.fori_loop(1, nx * ny, one, 0)

    def shared(table, k):
        arrive(table.at[pl.ds(0, nx * ny - 1)], k)
        total = jnp.sum(table[...], axis=0)
        return total[:, 0:1], total[:, 64:65]

    share(num, den, esend, ebuf, 4)
    h_w = h_local + correction(coef_h)
    s_w = w + correction(coef_s)
    fields[0] = h_w
    fields[1] = s_w

    for f in range(2):
        bface[f, 0:8, :] = fields[f, pl.ds(0, 8, stride=16), :]
        bface[f, 8:16, :] = fields[f, pl.ds(15, 8, stride=16), :]
    send(fields.at[:, pl.ds(0, 16)], bhalo.at[:, pl.ds(16, 16)], 5, device(-1, 0))
    send(fields.at[:, pl.ds(112, 16)], bhalo.at[:, pl.ds(0, 16)], 5, device(1, 0))
    send(bface.at[:, pl.ds(0, 8)], bhalo.at[:, pl.ds(40, 8)], 5, device(0, -1))
    send(bface.at[:, pl.ds(8, 8)], bhalo.at[:, pl.ds(32, 8)], 5, device(0, 1))
    flat = mm(jnp.concatenate([h_w, s_w], axis=1), const["down_one_z"][...])
    one = mm(const["down_one"][...], jnp.concatenate([flat[:, :128], flat[:, 128:]], axis=0))
    one_s[...] = one[:ROWS_ONE]
    one_r[ROWS_ONE:STACK_ONE, :] = one[ROWS_ONE:]
    for t in NEAR:
        at, block = BLOCKS_ONE[t]
        n = pad8(len(block))
        send(one_s.at[pl.ds(at, n)], one_r.at[pl.ds(at, n)], 6, device(*t))
    flat = mm(one[ROWS_ONE:], const["down_two_z"][...])
    two = mm(const["down_two"][...], jnp.concatenate([flat[:, :128], flat[:, 128:]], axis=0))
    two_s[...] = two[:ROWS_TWO]
    two_r[ROWS_TWO:STACK_TWO, :] = two[ROWS_TWO:]
    for t in FAR:
        at, block = BLOCKS_TWO[t]
        n = pad8(len(block))
        send(two_s.at[pl.ds(at, n)], two_r.at[pl.ds(at, n)], 7, device(*t))

    arrive(one_s, 6)
    level1 = one_r[...]
    level1_z = mm(level1, const["one_z"][...])
    arrive(two_s, 7)
    flat = mm(two_r[...], const["sweep_two_z"][...])
    x2 = mm(
        const["sweep_two"][...],
        jnp.concatenate([flat[:, :128], flat[:, 128:256], flat[:, 256:]], axis=0),
    )
    flat = mm(x2, const["up_one_z"][...])
    x1 = mm(const["up_one"][...], jnp.concatenate([level1, level1_z, flat[:, :128], flat[:, 128:]], axis=0))
    num, den = shared(ebuf, 4)
    energy = num / den
    residual = h_w - energy * s_w
    x1 = x1 - energy * pltpu.roll(x1, 64, 1)
    flat = mm(x1, const["up_zero_z"][...])
    arrive(bhalo, 5)
    faces = bhalo[0] - energy * bhalo[1]
    direction = mm(
        const["up_zero"][...],
        jnp.concatenate([residual, flat[:, :128], flat[:, 128:], faces], axis=0),
    ) + mm(residual, const["zero_z"][...])

    dirs[...] = direction
    for j in range(3):
        stage[48 + 8 * j : 56 + 8 * j, :] = dirs[pl.ds(j, 8, stride=16), :]
        stage[72 + 8 * j : 80 + 8 * j, :] = dirs[pl.ds(13 + j, 8, stride=16), :]
    send(dirs.at[pl.ds(0, 48)], halo2.at[pl.ds(48, 48)], 8, device(-1, 0))
    send(dirs.at[pl.ds(80, 48)], halo2.at[pl.ds(0, 48)], 8, device(1, 0))
    send(stage.at[pl.ds(48, 24)], halo2.at[pl.ds(120, 24)], 8, device(0, -1))
    send(stage.at[pl.ds(72, 24)], halo2.at[pl.ds(96, 24)], 8, device(0, 1))
    q_own = overlaps(direction)
    qbuf2[...] = q_own
    ring_send(qbuf2, qrecv2, 9)
    change = mm(const["kin_own"][...], direction) + mm(direction, const["kin_z"][...])
    change = change + (potential - energy) * direction
    arrive(halo2, 8)
    change = change + mm(const["kin_side"][...], halo2[...])
    arrive(qrecv2, 9)
    q = gather_overlaps(q_own, qrecv2)
    change = change + correction(coefficients(q, 0) - energy * coefficients(q, 1))
    along = total_of(jnp.sum(residual * change, axis=0, keepdims=True))
    square = total_of(jnp.sum(change * change, axis=0, keepdims=True))
    share(along, square, lsend, lbuf, 10)

    left(infos.at[pl.ds(0, 8)], 0)
    left(halo, 1)
    if nb > 1:
        left(pots.at[pl.ds(0, nb - 1)], 2)
    left(qrecv, 3)
    left(ebuf.at[pl.ds(0, nx * ny - 1)], 4)
    left(bhalo, 5)
    left(one_s, 6)
    left(two_s, 7)
    left(halo2, 8)
    left(qrecv2, 9)
    left(lbuf.at[pl.ds(0, nx * ny - 1)], 10)

    along, square = shared(lbuf, 10)
    step = -along / square
    bands_ref[...] = w + step * direction
    resid_ref[...] = residual + step * change
    energy_ref[0] = energy[0, 0]


def solution(mesh):
    shape = tuple(mesh.shape[name] for name in ("band", "dx", "dy"))
    nb, nx, ny = shape
    held = constants()

    def on_device(wave_bands, potential, atom_offsets, proj_counts, dh_matrix, ds_matrix):
        vmem = pl.BlockSpec(memory_space=pltpu.VMEM)
        smem = pl.BlockSpec(memory_space=pltpu.SMEM)
        v = lambda *dims: pltpu.VMEM(dims, F32)
        bands, resid, energy = pl.pallas_call(
            functools.partial(kernel, shape),
            out_shape=(
                jax.ShapeDtypeStruct((128, 128), F32),
                jax.ShapeDtypeStruct((128, 128), F32),
                jax.ShapeDtypeStruct((1,), F32),
            ),
            in_specs=[vmem, vmem, smem, smem, vmem, vmem] + [vmem] * len(NAMES),
            out_specs=(vmem, vmem, smem),
            scratch_shapes=[
                v(96, 128),
                v(144, 128),
                v(144, 128),
                v(128, 128),
                v(8, 256),
                v(16, 8, 256),
                v(2, 128, 128),
                v(nb, 128, 128),
                v(8, 128),
                v(24, 8, 128),
                v(8, 128),
                v(24, 8, 128),
                v(2, 128, 128),
                v(2, 16, 128),
                v(2, 48, 128),
                v(ROWS_ONE, 128),
                v(STACK_ONE, 128),
                v(ROWS_TWO, 128),
                v(STACK_TWO, 128),
                v(1, 128),
                v(nx * ny, 1, 128),
                v(1, 128),
                v(nx * ny, 1, 128),
                v(4, 128, 128),
                v(5, 128, 128),
                pltpu.SemaphoreType.DMA((11,)),
                pltpu.SemaphoreType.DMA((11,)),
            ],
            compiler_params=pltpu.CompilerParams(
                collective_id=0, has_side_effects=True, vmem_limit_bytes=40 << 20
            ),
        )(
            wave_bands.reshape(128, 128),
            potential.reshape(128, 32),
            atom_offsets,
            proj_counts,
            dh_matrix.reshape(ATOMS, 9, 9),
            ds_matrix.reshape(ATOMS, 9, 9),
            *[held[name] for name in NAMES],
        )
        return bands.reshape(1, CX, CY, NZ), resid.reshape(1, CX, CY, NZ), energy

    return jax.shard_map(
        on_device,
        mesh=mesh,
        in_specs=(
            P("band", "dx", "dy", None),
            P("dx", "dy", "band"),
            P("dx", "dy", None, None),
            P("dx", "dy", None),
            P("dx", "dy", None, None, None),
            P("dx", "dy", None, None, None),
        ),
        out_specs=(P("band", "dx", "dy", None), P("band", "dx", "dy", None), P("band")),
        check_vma=False,
    )
```

profile of v0, /device:TPU:1, one launch (start us, length us, event | category | flops | bytes accessed | tf_op | source)
XLA Modules:
  0.0 65.4 jit_solution(5416056754030187501)
XLA Ops:
  0.6 0.0 copy-start.5
  0.6 0.8 %copy.26.refs_2_ = s32[1,1,4,3]{3,2,1,0:T(4,128)S(1)} copy(s32[1,1,4,3]{2,1,3,0:T(1,128)} %param.23) | data formatting | bytes 96 | tf_op args[2]
  1.4 0.7 %copy_bitcast_fusion = (f32[4,9,9]{2,1,0:T(8,128)S(1)}, f32[4,9,9]{2,1,0:T(8,128)S(1)}) fusion(f32[1,1,4,9,9]{4,2,3,1,0:T(4,128)} %param.26, f32[1,1,4,9,9]{4,2,3,1,0:T(4,128)} %param.25), kind=kLoop, calls=%fused_computation | loop fusion | bytes 5184 | tf_op jit(solution)/shard_map/reshape | solution.py:650
  2.2 0.0 copy-start.17
  2.2 0.0 copy-done.5
  2.2 0.6 copy-done.17
  2.8 0.0 copy-start
  2.8 0.9 %copy-done = f32[256,256]{1,0:T(8,128)S(1)} copy-done((f32[256,256]{1,0:T(8,128)S(1)}, f32[256,256]{1,0:T(8,128)}, u32[]{:S(2)}) %copy-start) | copy-done | bytes 262168
  3.8 0.0 copy-start.1
  3.8 0.9 %copy-done.1 = f32[240,256]{1,0:T(8,128)S(1)} copy-done((f32[240,256]{1,0:T(8,128)S(1)}, f32[240,256]{1,0:T(8,128)}, u32[]{:S(2)}) %copy-start.1) | copy-done | bytes 245784
  4.7 0.0 copy-start.2
  4.7 0.9 %copy-done.2 = f32[128,304]{1,0:T(8,128)S(1)} copy-done((f32[128,304]{1,0:T(8,128)S(1)}, f32[128,304]{1,0:T(8,128)}, u32[]{:S(2)}) %copy-start.2) | copy-done | bytes 155672
  5.7 0.0 copy-start.3
  5.7 0.9 %copy-done.3 = f32[128,384]{1,0:T(8,128)S(1)} copy-done((f32[128,384]{1,0:T(8,128)S(1)}, f32[128,384]{1,0:T(8,128)}, u32[]{:S(2)}) %copy-start.3) | copy-done | bytes 196632
  6.6 0.0 copy-start.4
  6.6 0.9 %copy-done.4 = f32[64,528]{1,0:T(8,128)S(1)} copy-done((f32[64,528]{1,0:T(8,128)S(1)}, f32[64,528]{1,0:T(8,128)}, u32[]{:S(2)}) %copy-start.4) | copy-done | bytes 135192
  7.5 0.0 copy-start.6
  7.5 0.9 %copy-done.6 = f32[128,256]{1,0:T(8,128)S(1)} copy-done((f32[128,256]{1,0:T(8,128)S(1)}, f32[128,256]{1,0:T(8,128)}, u32[]{:S(2)}) %copy-start.6) | copy-done | bytes 131096
  8.4 0.0 copy-start.7
  8.4 0.9 %copy-done.7 = f32[128,256]{1,0:T(8,128)S(1)} copy-done((f32[128,256]{1,0:T(8,128)S(1)}, f32[128,256]{1,0:T(8,128)}, u32[]{:S(2)}) %copy-start.7) | copy-done | bytes 131096
  9.3 0.9 %copy-done.8 = f32[128,144]{1,0:T(8,128)S(1)} copy-done((f32[128,144]{1,0:T(8,128)S(1)}, f32[128,144]{1,0:T(8,128)}, u32[]{:S(2)}) %copy-start.8) | copy-done | bytes 73752
  10.2 0.9 %copy-done.9 = f32[232,128]{1,0:T(8,128)S(1)} copy-done((f32[232,128]{1,0:T(8,128)S(1)}, f32[232,128]{1,0:T(8,128)}, u32[]{:S(2)}) %copy-start.9) | copy-done | bytes 118808
  11.1 0.9 %copy-done.10 = f32[24,696]{1,0:T(8,128)S(1)} copy-done((f32[24,696]{1,0:T(8,128)S(1)}, f32[24,696]{1,0:T(8,128)}, u32[]{:S(2)}) %copy-start.10) | copy-done | bytes 66840
  12.0 0.8 %copy-done.11 = f32[1,8,16,128]{3,2,1,0:T(8,128)S(1)} copy-done((f32[1,8,16,128]{3,2,1,0:T(8,128)S(1)}, f32[1,8,16,128]{3,2,1,0:T(8,128)}, u32[]{:S(2)}) %copy-start.11) | copy-done | bytes 65560
  12.9 0.8 %copy-done.12 = f32[8,16,32]{2,1,0:T(8,128)S(1)} copy-done((f32[8,16,32]{2,1,0:T(8,128)S(1)}, f32[8,16,32]{2,1,0:T(8,128)}, u32[]{:S(2)}) %copy-start.12) | copy-done | bytes 16408
  13.7 0.8 %copy-done.13 = f32[128,128]{1,0:T(8,128)S(1)} copy-done((f32[128,128]{1,0:T(8,128)S(1)}, f32[128,128]{1,0:T(8,128)}, u32[]{:S(2)}) %copy-start.13) | copy-done | bytes 65560
  14.5 0.8 %copy-done.14 = f32[128,128]{1,0:T(8,128)S(1)} copy-done((f32[128,128]{1,0:T(8,128)S(1)}, f32[128,128]{1,0:T(8,128)}, u32[]{:S(2)}) %copy-start.14) | copy-done | bytes 65560
  15.4 0.8 %copy-done.15 = f32[128,128]{1,0:T(8,128)S(1)} copy-done((f32[128,128]{1,0:T(8,128)S(1)}, f32[128,128]{1,0:T(8,128)}, u32[]{:S(2)}) %copy-start.15) | copy-done | bytes 65560
  16.2 0.8 %copy-done.16 = f32[128,128]{1,0:T(8,128)S(1)} copy-done((f32[128,128]{1,0:T(8,128)S(1)}, f32[128,128]{1,0:T(8,128)}, u32[]{:S(2)}) %copy-start.16) | copy-done | bytes 65560
  17.1 45.3 %shard_map.220 = (f32[128,128]{1,0:T(8,128)S(1)}, f32[128,128]{1,0:T(8,128)S(1)}, f32[1]{0:T(128)}) custom-call(f32[128,128]{1,0:T(8,128)S(1)} %bitcast.8, f32[128,32]{1,0:T(8,128)S(1)} %bitcast.9, s32[1,1,4,3]{3,2,1,0:T(4,128)S(1)} %copy.26.refs_2_, s32[1,1,4]{2,1,0:T(1,128)S(1)} %copy-done.17, f32[4,9,9]{2,1,0:T(8,128)S(1)} %get-tuple-element.10.refs_4_, ...), custom_call_target="tpu_custom_call" | custom-call | tf_op jit(solution)/shard_map/pallas_call | solution.py:603
  62.3 0.6 copy.32
  63.0 0.6 copy.33
  (9 shorter events, 0.0 us)
Async XLA Ops:
  0.6 1.6 %copy-start.5 = (f32[128,256]{1,0:T(8,128)S(1)}, f32[128,256]{1,0:T(8,128)}, u32[]{:S(2)}) copy-start(f32[128,256]{1,0:T(8,128)} %constant.44.clone.refs_20_) | copy-start | bytes 393220
  2.2 0.7 %copy-start.17 = (s32[1,1,4]{2,1,0:T(1,128)S(1)}, s32[1,1,4]{2,1,0:T(1,128)}, u32[]{:S(2)}) copy-start(s32[1,1,4]{2,1,0:T(1,128)} %refs_3_.1) | copy-start | bytes 52
  2.8 0.9 %copy-start = (f32[256,256]{1,0:T(8,128)S(1)}, f32[256,256]{1,0:T(8,128)}, u32[]{:S(2)}) copy-start(f32[256,256]{1,0:T(8,128)} %constant.34.clone.refs_10_) | copy-start | bytes 786436
  3.8 0.9 %copy-start.1 = (f32[240,256]{1,0:T(8,128)S(1)}, f32[240,256]{1,0:T(8,128)}, u32[]{:S(2)}) copy-start(f32[240,256]{1,0:T(8,128)} %constant.33.clone.refs_9_) | copy-start | bytes 737284
  4.7 0.9 %copy-start.2 = (f32[128,304]{1,0:T(8,128)S(1)}, f32[128,304]{1,0:T(8,128)}, u32[]{:S(2)}) copy-start(f32[128,304]{1,0:T(8,128)} %constant.42.clone.refs_18_) | copy-start | bytes 466948
  5.7 0.9 %copy-start.3 = (f32[128,384]{1,0:T(8,128)S(1)}, f32[128,384]{1,0:T(8,128)}, u32[]{:S(2)}) copy-start(f32[128,384]{1,0:T(8,128)} %constant.38.clone.refs_14_) | copy-start | bytes 589828
  6.6 0.9 %copy-start.4 = (f32[64,528]{1,0:T(8,128)S(1)}, f32[64,528]{1,0:T(8,128)}, u32[]{:S(2)}) copy-start(f32[64,528]{1,0:T(8,128)} %constant.39.clone.refs_15_) | copy-start | bytes 405508
  7.5 0.9 %copy-start.6 = (f32[128,256]{1,0:T(8,128)S(1)}, f32[128,256]{1,0:T(8,128)}, u32[]{:S(2)}) copy-start(f32[128,256]{1,0:T(8,128)} %constant.41.clone.refs_17_) | copy-start | bytes 393220
  8.4 0.9 %copy-start.7 = (f32[128,256]{1,0:T(8,128)S(1)}, f32[128,256]{1,0:T(8,128)}, u32[]{:S(2)}) copy-start(f32[128,256]{1,0:T(8,128)} %constant.36.clone.refs_12_) | copy-start | bytes 393220
  9.3 0.9 %copy-start.8 = (f32[128,144]{1,0:T(8,128)S(1)}, f32[128,144]{1,0:T(8,128)}, u32[]{:S(2)}) copy-start(f32[128,144]{1,0:T(8,128)} %constant.31.clone.refs_7_) | copy-start | bytes 221188
  10.2 0.9 %copy-start.9 = (f32[232,128]{1,0:T(8,128)S(1)}, f32[232,128]{1,0:T(8,128)}, u32[]{:S(2)}) copy-start(f32[232,128]{1,0:T(8,128)} %constant.35.clone.refs_11_) | copy-start | bytes 356356
  11.1 0.9 %copy-start.10 = (f32[24,696]{1,0:T(8,128)S(1)}, f32[24,696]{1,0:T(8,128)}, u32[]{:S(2)}) copy-start(f32[24,696]{1,0:T(8,128)} %constant.37.clone.refs_13_) | copy-start | bytes 200452
  12.0 0.8 %copy-start.11 = (f32[1,8,16,128]{3,2,1,0:T(8,128)S(1)}, f32[1,8,16,128]{3,2,1,0:T(8,128)}, u32[]{:S(2)}) copy-start(f32[1,8,16,128]{3,2,1,0:T(8,128)} %param.21) | copy-start | bytes 196612
  12.9 0.8 %copy-start.12 = (f32[8,16,32]{2,1,0:T(8,128)S(1)}, f32[8,16,32]{2,1,0:T(8,128)}, u32[]{:S(2)}) copy-start(f32[8,16,32]{2,1,0:T(8,128)} %param.22) | copy-start | bytes 49156
  13.7 0.8 %copy-start.13 = (f32[128,128]{1,0:T(8,128)S(1)}, f32[128,128]{1,0:T(8,128)}, u32[]{:S(2)}) copy-start(f32[128,128]{1,0:T(8,128)} %constant.43.clone.refs_19_) | copy-start | bytes 196612
  14.5 0.8 %copy-start.14 = (f32[128,128]{1,0:T(8,128)S(1)}, f32[128,128]{1,0:T(8,128)}, u32[]{:S(2)}) copy-start(f32[128,128]{1,0:T(8,128)} %constant.40.clone.refs_16_) | copy-start | bytes 196612
  15.4 0.8 %copy-start.15 = (f32[128,128]{1,0:T(8,128)S(1)}, f32[128,128]{1,0:T(8,128)}, u32[]{:S(2)}) copy-start(f32[128,128]{1,0:T(8,128)} %constant.32.clone.refs_8_) | copy-start | bytes 196612
  16.2 0.8 %copy-start.16 = (f32[128,128]{1,0:T(8,128)S(1)}, f32[128,128]{1,0:T(8,128)}, u32[]{:S(2)}) copy-start(f32[128,128]{1,0:T(8,128)} %constant.30.clone.refs_6_) | copy-start | bytes 196612
where the time goes:
time: 66.1 us; the launch traced here: 65.4 us
  Pallas kernels  45.3 us (69%)
  local copies, waits for them, and re-layouts  17.6 us (27%)
  between operations  2.5 us (4%)
    pallas_call x1, Pallas kernels, on_device(): pl.pallas_call(functools.partial(kernel, shape), out_shape=(jax.ShapeDtyp...  45.3 us
    unnamed x39, local copies, waits for them, and re-layouts  16.9 us

commit v1 on v0

--- a/solution.py
+++ b/solution.py
@@ -9,8 +9,8 @@
 from jax.sharding import PartitionSpec as P
 
 MESH = pl.DeviceIdType.MESH
-HIGHEST = lax.Precision.HIGHEST
 F32 = jnp.float32
+BF16 = jnp.bfloat16
 
 STENCIL = (-49.0 / 18.0, 1.5, -0.15, 1.0 / 90.0)
 RELAXATION = 2.0 / 3.0
@@ -101,7 +101,7 @@
 
 NEAR = [(a, b) for a in (-1, 0, 1) for b in (-1, 0, 1) if (a, b) != (0, 0)]
 FAR = [(a, b) for a in (-2, -1, 0, 1, 2) for b in (-1, 0, 1) if (a, b) != (0, 0)]
-RING = [(a, b) for a in range(-2, 3) for b in range(-2, 3) if (a, b) != (0, 0)]
+GREET = [(a, b) for a in (-1, 0, 1) for b in (-2, -1, 0, 1, 2) if (a, b) != (0, 0)]
 
 
 def blocks(own, wide, step, targets):
@@ -117,13 +117,13 @@
 BLOCKS_ONE, ROWS_ONE = blocks(ONE, ONE_WIDE, (4, 8), NEAR)
 BLOCKS_TWO, ROWS_TWO = blocks(TWO, TWO_WIDE, (2, 4), FAR)
 OWN_ONE = pad8(len(ONE))
-OWN_TWO = pad8(len(TWO))
+OWN_TWO = 32
 STACK_ONE = ROWS_ONE + OWN_ONE
 STACK_TWO = ROWS_TWO + OWN_TWO
 
 
 def senders(table, rows, own):
-    m = np.zeros((rows + pad8(len(own)), len(own)))
+    m = np.zeros((rows + (OWN_ONE if own is ONE else OWN_TWO), len(own)))
     for at, block in table.values():
         m[at : at + len(block)] = pick(block, own)
     m[rows : rows + len(own)] = np.eye(len(own))
@@ -131,7 +131,7 @@
 
 
 def receivers(table, rows, own, wide, step):
-    m = np.zeros((len(wide), rows + pad8(len(own))))
+    m = np.zeros((len(wide), rows + (OWN_ONE if own is ONE else OWN_TWO)))
     for t, (at, block) in table.items():
         here = [(i - step[0] * t[0], j - step[1] * t[1]) for i, j in block]
         m[:, at : at + len(block)] = pick(wide, here)
@@ -171,8 +171,6 @@
     one_along = avg @ pick(ring0, FINE) * SIDE[0]
     send = senders(BLOCKS_ONE, ROWS_ONE, ONE)
     c["down_one"] = np.concatenate([send @ one_plane, send @ one_along], axis=1)
-    half = halve_z(NZ)
-    c["down_one_z"] = np.concatenate([both(half), both(along_z(NZ) @ half)], axis=1)
 
     ring1 = cells(-2, 6, -2, 10)
     avg = average(TWO, ring1)
@@ -180,11 +178,11 @@
     two_along = avg @ pick(ring1, ONE) * SIDE[1]
     send = senders(BLOCKS_TWO, ROWS_TWO, TWO)
     c["down_two"] = np.concatenate(
-        [grown(send @ two_plane, STACK_TWO, OWN_ONE), grown(send @ two_along, STACK_TWO, OWN_ONE)], axis=1
-    )
-    half = halve_z(64)
-    c["down_two_z"] = np.concatenate(
-        [grown(both(half), 128, 128), grown(both(along_z(64) @ half), 128, 128)], axis=1
+        [send @ two @ one for two in (two_plane, two_along) for one in (one_plane, one_along)], axis=1
+    )
+    h0, n0, h1, n1 = halve_z(NZ), along_z(NZ), halve_z(64), along_z(64)
+    c["down_z"] = np.concatenate(
+        [both(m) for m in (h0, n0 @ h0, h0 @ h1, n0 @ h0 @ h1, h0 @ n1 @ h1, n0 @ h0 @ n1 @ h1)], axis=1
     )
 
     take = receivers(BLOCKS_TWO, ROWS_TWO, TWO, TWO_WIDE, (2, 4))
@@ -213,13 +211,13 @@
             [
                 g * (4.0 / 3.0 * here + k * n1) @ take,
                 g * k * here @ take,
-                (here / 3.0 + k * n1) @ up,
-                k * here @ up,
+                grown((here / 3.0 + k * n1) @ up, len(ONE), OWN_TWO),
+                grown(k * here @ up, len(ONE), OWN_TWO),
             ],
             axis=1,
         ),
         OWN_ONE,
-        2 * STACK_ONE + 2 * len(TWO),
+        2 * STACK_ONE + 2 * OWN_TWO,
     )
     nz = along_z(64)
     c["one_z"] = both(nz)
@@ -246,36 +244,41 @@
     )
     nz = along_z(NZ)
     double = double_z(64)
-    c["zero_z"] = g * k * nz
+    c["zero_z"] = nz
     c["up_zero_z"] = np.concatenate([grown(double, 128, 128), grown(double @ nz, 128, 128)], axis=1)
-    return {name: m.astype(np.float32) for name, m in c.items()}
-
-
-NAMES = (
-    "kin_own",
-    "kin_side",
-    "kin_z",
-    "down_one",
-    "down_one_z",
-    "down_two",
-    "down_two_z",
-    "sweep_two",
-    "sweep_two_z",
-    "up_one",
-    "one_z",
-    "up_one_z",
-    "up_zero",
-    "zero_z",
-    "up_zero_z",
-)
-
-
-def mm(a, b):
-    return lax.dot_general(a, b, (((1,), (0,)), ((), ())), precision=HIGHEST, preferred_element_type=F32)
-
-
-def mm_t(a, b):
-    return lax.dot_general(a, b, (((1,), (1,)), ((), ())), precision=HIGHEST, preferred_element_type=F32)
+    return c
+
+
+def packed():
+    table, parts, at = {}, [], 0
+    for name, m in constants().items():
+        rows, cols = m.shape
+        rows = (rows + 15) // 16 * 16
+        m = grown(m, rows, (cols + 127) // 128 * 128).astype(np.float32)
+        high = m.astype(jnp.bfloat16)
+        low = (m - high.astype(np.float32)).astype(jnp.bfloat16)
+        exact = not low.astype(np.float32).any()
+        places = []
+        for part in (high,) if exact else (high, low):
+            tiles = [part[:, t : t + 128] for t in range(0, m.shape[1], 128)]
+            places.append([at + n * rows for n in range(len(tiles))])
+            at += rows * len(tiles)
+            parts += tiles
+        table[name] = (rows, cols, places)
+    return table, np.concatenate(parts, axis=0)
+
+
+def dot(a, b):
+    return lax.dot_general(a, b, (((1,), (0,)), ((), ())), preferred_element_type=F32)
+
+
+def split(x):
+    high = x.astype(BF16)
+    return high, (x - high.astype(F32)).astype(BF16)
+
+
+def dot3(a, b):
+    return dot(a[0], b[0]) + dot(a[1], b[0]) + dot(a[0], b[1])
 
 
 def projector_of(p, right):
@@ -284,17 +287,42 @@
     return jnp.where(right, right_of, left_of)
 
 
-def kernel(shape, *refs):
+def kernel(shape, table, *refs):
     nb, nx, ny = shape
-    w_ref, pot_ref, offs_ref, cnt_ref, dh_ref, ds_ref = refs[:6]
-    const = dict(zip(NAMES, refs[6 : 6 + len(NAMES)]))
-    outs = refs[6 + len(NAMES) : 9 + len(NAMES)]
-    bands_ref, resid_ref, energy_ref = outs
     (
+        w_in, pot_in, offs_in, cnt_in, dh_in, ds_in, const_in,
+        bands_ref, resid_ref, energy_ref,
+        w_ref, pot_ref, offs_ref, cnt_ref, d_ref, const,
         stage, halo, halo2, dirs, info, infos, infot, pots, qbuf, qrecv, qbuf2, qrecv2,
-        fields, bface, bhalo, one_s, one_r, two_s, two_r, esend, ebuf, lsend, lbuf, zfun, wfun,
-        ssem, rsem,
-    ) = refs[9 + len(NAMES) :]
+        fields, bface, bhalo, one_s, one_r, two_s, two_r, esend, ebuf, lsend, lbuf, zfun, zturn, wfun,
+        lsem, ssem, rsem,
+    ) = refs
+    loads = [
+        pltpu.make_async_copy(src, dst, lsem.at[n])
+        for n, (src, dst) in enumerate(
+            (
+                (offs_in, offs_ref), (cnt_in, cnt_ref), (dh_in, d_ref.at[0]), (ds_in, d_ref.at[1]),
+                (w_in, w_ref), (pot_in, pot_ref), (const_in, const),
+            )
+        )
+    ]
+    for load in loads:
+        load.start()
+
+    def held(name):
+        rows, cols, places = table[name]
+        return [jnp.concatenate([const[at : at + rows, :] for at in tiles], axis=1)[:, :cols] for tiles in places]
+
+    def from_left(name, x):
+        c, (high, low) = held(name), split(x)
+        total = dot(c[0], high) + dot(c[0], low)
+        return total + dot(c[1], high) if len(c) > 1 else total
+
+    def from_right(x, name):
+        c, (high, low) = held(name), split(x)
+        total = dot(high, c[0]) + dot(low, c[0])
+        return total + dot(high, c[1]) if len(c) > 1 else total
+
     ib, ix, iy = lax.axis_index("band"), lax.axis_index("dx"), lax.axis_index("dy")
 
     def device(a, b, band=0):
@@ -317,43 +345,47 @@
     infos[...] = jnp.zeros_like(infos)
     barrier = pltpu.get_barrier_semaphore()
 
-    def greet(i, carry):
-        a, b = i // ny, lax.rem(i, ny)
+    for a, b in GREET:
         pl.semaphore_signal(barrier, inc=1, device_id=device(a, b), device_id_type=MESH)
-        return carry
-
-    lax.fori_loop(1, nx * ny, greet, 0)
     for i in range(1, nb):
         pl.semaphore_signal(barrier, inc=1, device_id=device(0, 0, i), device_id_type=MESH)
 
+    for load in loads[:6]:
+        load.wait()
     for j in range(3):
         stage[8 * j : 8 * j + 8, :] = w_ref[pl.ds(j, 8, stride=16), :]
         stage[24 + 8 * j : 32 + 8 * j, :] = w_ref[pl.ds(13 + j, 8, stride=16), :]
     row = lax.broadcasted_iota(jnp.int32, (128, 128), 0)
     lane = lax.broadcasted_iota(jnp.int32, (1, 128), 1)
     place = (lax.broadcasted_iota(jnp.int32, (32, 128), 0) + 32 * ib == lax.broadcasted_iota(jnp.int32, (32, 128), 1)).astype(F32)
-    pots[ib] = mm(pot_ref[...], place)
+    place = place.astype(BF16)
+    high, low = split(pot_ref[...])
+    rest = pot_ref[...] - high.astype(F32) - low.astype(F32)
+    pots[ib] = dot(high, place) + dot(low, place) + dot(rest.astype(BF16), place)
     crossed, p_from, p_to = lane // 40, (lane // 8) % 5, lane % 8
-    which = lax.broadcasted_iota(jnp.int32, (9, 128), 0)
     lane4 = lax.broadcasted_iota(jnp.int32, (ATOMS, 128), 1)
     atom4 = lax.broadcasted_iota(jnp.int32, (ATOMS, 128), 0)
     for right in (0, 1):
         j_of = projector_of(p_from, (crossed != right))
         i_of = projector_of(p_to, lane * 0 + right == 1)
-        chosen = ((which == i_of) & (lane < 80)).astype(F32)
+        chosen = [((i_of == i) & (lane < 80)).astype(F32) for i in range(9)]
+        from_j = [(j_of == j).astype(F32) for j in range(9)]
         place_of = jnp.zeros((ATOMS, 128), F32)
         for k in range(ATOMS):
-            for m, v in enumerate((offs_ref[0, 0, k, 0], offs_ref[0, 0, k, 1], offs_ref[0, 0, k, 2], cnt_ref[0, 0, k])):
+            for m, v in enumerate((offs_ref[0, 0, 0, k], offs_ref[0, 1, 0, k], offs_ref[0, 2, 0, k], cnt_ref[0, 0, k])):
                 place_of = jnp.where((atom4 == k) & (lane4 == 80 + m), v.astype(F32), place_of)
-        for n, ref in enumerate((dh_ref, ds_ref)):
-            full = jnp.zeros((ATOMS, 9, 128), F32)
-            for j in range(9):
-                full = full + ref[:, :, j : j + 1] * (j_of == j).astype(F32)[None]
-            rows = jnp.sum(full * chosen[None], axis=1)
-            info[4 * right : 4 * right + 4, 128 * n : 128 * n + 128] = rows + place_of if n == 0 else rows
+        for n in range(2):
+            rows = place_of if n == 0 else jnp.zeros((ATOMS, 128), F32)
+            for i in range(9):
+                of_i = d_ref[n, i]
+                full = of_i[:, 0:1] * from_j[0]
+                for j in range(1, 9):
+                    full = full + of_i[:, j : j + 1] * from_j[j]
+                rows = rows + full * chosen[i]
+            info[4 * right : 4 * right + 4, 128 * n : 128 * n + 128] = rows
     infos[slot] = info[...]
 
-    pl.semaphore_wait(barrier, nx * ny - 1 + nb - 1)
+    pl.semaphore_wait(barrier, len(GREET) + nb - 1)
 
     for a, b in NEAR:
         send(info, infos.at[slot], 0, device(a, b))
@@ -364,7 +396,8 @@
     for i in range(1, nb):
         send(pots.at[ib], pots.at[ib], 2, device(0, 0, i))
     w = w_ref[...]
-    kin = mm(const["kin_own"][...], w) + mm(w, const["kin_z"][...])
+    loads[6].wait()
+    kin = from_left("kin_own", w) + from_right(w, "kin_z")
 
     arrive(infos.at[pl.ds(0, 8)], 0)
     for n in range(2):
@@ -389,10 +422,11 @@
 
     rz, qz, (zs, zp, zd) = bells(NZ, centre_z)
     zp, zd = zp * (1.0 / 2.2), zd * (1.0 / 5.76)
-    zfun[0] = jnp.where(right_lane, rz * zp, zs)
-    zfun[1] = jnp.where(right_lane, rz * zd, zp)
-    zfun[2] = jnp.where(right_lane, qz * zd, zd)
-    zfun[3] = zd
+    zs = (
+        jnp.where(right_lane, rz * zp, zs), jnp.where(right_lane, rz * zd, zp), jnp.where(right_lane, qz * zd, zd), zd,
+    )
+    for n, v in enumerate(split(jnp.concatenate(zs, axis=1))):
+        zfun[n] = v
     rx, qx, (xs, xp, xd) = bells(CX, centre_x)
     ry, qy, (ys, yp, yd) = bells(CY, centre_y)
     pairs = (
@@ -411,20 +445,20 @@
     tile_of = (0, 1, 1, 2, 3)
 
     def overlaps(field):
-        part = [mm(field, zfun[t]) for t in range(4)]
-        rows = [jnp.sum(part[tile_of[p]] * wfun[p], axis=0, keepdims=True) for p in range(5)]
+        part = dot3(split(field), (zfun[0], zfun[1]))
+        rows = [
+            jnp.sum(part[:, 128 * tile_of[p] : 128 * tile_of[p] + 128] * wfun[p], axis=0, keepdims=True) for p in range(5)
+        ]
         return jnp.concatenate(rows + [jnp.zeros((3, 128), F32)], axis=0)
 
     keep_x = {-2: (rel_x == -1).astype(F32), 2: (rel_x == 1).astype(F32)}
-    keep_y = {-2: (rel_y == -1).astype(F32), 2: (rel_y == 1).astype(F32)}
 
     def gather_overlaps(own, ref):
         total = None
         for a in range(-2, 3):
             line = None
-            for b in range(-2, 3):
-                v = own if (a, b) == (0, 0) else ref[RING.index((a, b))]
-                v = v * keep_y[b] if b in keep_y else v
+            for b in (-1, 0, 1):
+                v = own if (a, b) == (0, 0) else ref[FAR.index((a, b))]
                 line = v if line is None else line + v
             line = line * keep_x[a] if a in keep_x else line
             total = line if total is None else total + line
@@ -440,28 +474,29 @@
                 total = term if total is None else total + term
         return total * active
 
-    def correction(coefs):
-        total = None
-        for t in range(4):
-            weight = None
-            for p in range(5):
-                if tile_of[p] == t:
-                    term = wfun[p] * coefs[p : p + 1, :]
-                    weight = term if weight is None else weight + term
-            term = mm_t(weight, zfun[t])
-            total = term if total is None else total + term
-        return total
+    def weights(coefs):
+        tiles = [None] * 4
+        for p in range(5):
+            term = wfun[p] * coefs[p : p + 1, :]
+            t = tile_of[p]
+            tiles[t] = term if tiles[t] is None else tiles[t] + term
+        return jnp.concatenate(tiles, axis=1)
+
+    def correction(weight):
+        return dot3(split(weight), (zturn[0], zturn[1]))
 
     def ring_send(src, dst, k):
-        for a, b in RING:
-            send(src, dst.at[RING.index((-a, -b))], k, device(a, b))
+        for a, b in FAR:
+            send(src, dst.at[FAR.index((-a, -b))], k, device(a, b))
 
     q_own = overlaps(w)
     qbuf[...] = q_own
     ring_send(qbuf, qrecv, 3)
+    for n, v in enumerate(split(jnp.concatenate([jnp.swapaxes(z, 0, 1) for z in zs], axis=0))):
+        zturn[n] = v
 
     arrive(halo, 1)
-    kin = kin + mm(const["kin_side"][...], halo[...])
+    kin = kin + from_left("kin_side", halo[...])
     if nb > 1:
         arrive(pots.at[pl.ds(0, nb - 1)], 2)
     potential = pots[0]
@@ -496,9 +531,9 @@
         total = jnp.sum(table[...], axis=0)
         return total[:, 0:1], total[:, 64:65]
 
-    share(num, den, esend, ebuf, 4)
-    h_w = h_local + correction(coef_h)
-    s_w = w + correction(coef_s)
+    both_terms = correction(jnp.concatenate([weights(coef_h), weights(coef_s)], axis=0))
+    h_w = h_local + both_terms[:128]
+    s_w = w + both_terms[128:]
     fields[0] = h_w
     fields[1] = s_w
 
@@ -509,16 +544,19 @@
     send(fields.at[:, pl.ds(112, 16)], bhalo.at[:, pl.ds(0, 16)], 5, device(1, 0))
     send(bface.at[:, pl.ds(0, 8)], bhalo.at[:, pl.ds(40, 8)], 5, device(0, -1))
     send(bface.at[:, pl.ds(8, 8)], bhalo.at[:, pl.ds(32, 8)], 5, device(0, 1))
-    flat = mm(jnp.concatenate([h_w, s_w], axis=1), const["down_one_z"][...])
-    one = mm(const["down_one"][...], jnp.concatenate([flat[:, :128], flat[:, 128:]], axis=0))
+    flat = from_right(jnp.concatenate([h_w, s_w], axis=1), "down_z")
+    one = from_left("down_one", jnp.concatenate([flat[:, :128], flat[:, 128:256]], axis=0))
     one_s[...] = one[:ROWS_ONE]
     one_r[ROWS_ONE:STACK_ONE, :] = one[ROWS_ONE:]
     for t in NEAR:
         at, block = BLOCKS_ONE[t]
         n = pad8(len(block))
         send(one_s.at[pl.ds(at, n)], one_r.at[pl.ds(at, n)], 6, device(*t))
-    flat = mm(one[ROWS_ONE:], const["down_two_z"][...])
-    two = mm(const["down_two"][...], jnp.concatenate([flat[:, :128], flat[:, 128:]], axis=0))
+    lower, upper = flat[:, 256:384], flat[:, 384:]
+    two = from_left(
+        "down_two",
+        jnp.concatenate([lower, pltpu.roll(lower, 64, 1), upper, pltpu.roll(upper, 64, 1)], axis=0),
+    )
     two_s[...] = two[:ROWS_TWO]
     two_r[ROWS_TWO:STACK_TWO, :] = two[ROWS_TWO:]
     for t in FAR:
@@ -526,28 +564,26 @@
         n = pad8(len(block))
         send(two_s.at[pl.ds(at, n)], two_r.at[pl.ds(at, n)], 7, device(*t))
 
+    share(num, den, esend, ebuf, 4)
+
     arrive(one_s, 6)
     level1 = one_r[...]
-    level1_z = mm(level1, const["one_z"][...])
+    level1_z = from_right(level1, "one_z")
     arrive(two_s, 7)
-    flat = mm(two_r[...], const["sweep_two_z"][...])
-    x2 = mm(
-        const["sweep_two"][...],
-        jnp.concatenate([flat[:, :128], flat[:, 128:256], flat[:, 256:]], axis=0),
-    )
-    flat = mm(x2, const["up_one_z"][...])
-    x1 = mm(const["up_one"][...], jnp.concatenate([level1, level1_z, flat[:, :128], flat[:, 128:]], axis=0))
+    flat = from_right(two_r[...], "sweep_two_z")
+    x2 = from_left("sweep_two", jnp.concatenate([flat[:, :128], flat[:, 128:256], flat[:, 256:]], axis=0))
+    flat = from_right(x2, "up_one_z")
+    x1 = from_left("up_one", jnp.concatenate([level1, level1_z, flat[:, :128], flat[:, 128:]], axis=0))
     num, den = shared(ebuf, 4)
     energy = num / den
     residual = h_w - energy * s_w
     x1 = x1 - energy * pltpu.roll(x1, 64, 1)
-    flat = mm(x1, const["up_zero_z"][...])
+    flat = from_right(x1, "up_zero_z")
     arrive(bhalo, 5)
     faces = bhalo[0] - energy * bhalo[1]
-    direction = mm(
-        const["up_zero"][...],
-        jnp.concatenate([residual, flat[:, :128], flat[:, 128:], faces], axis=0),
-    ) + mm(residual, const["zero_z"][...])
+    direction = from_left(
+        "up_zero", jnp.concatenate([residual, flat[:, :128], flat[:, 128:], faces], axis=0)
+    ) + (GAIN[0] * SIDE[0]) * from_right(residual, "zero_z")
 
     dirs[...] = direction
     for j in range(3):
@@ -560,13 +596,13 @@
     q_own = overlaps(direction)
     qbuf2[...] = q_own
     ring_send(qbuf2, qrecv2, 9)
-    change = mm(const["kin_own"][...], direction) + mm(direction, const["kin_z"][...])
+    change = from_left("kin_own", direction) + from_right(direction, "kin_z")
     change = change + (potential - energy) * direction
     arrive(halo2, 8)
-    change = change + mm(const["kin_side"][...], halo2[...])
+    change = change + from_left("kin_side", halo2[...])
     arrive(qrecv2, 9)
     q = gather_overlaps(q_own, qrecv2)
-    change = change + correction(coefficients(q, 0) - energy * coefficients(q, 1))
+    change = change + correction(weights(coefficients(q, 0) - energy * coefficients(q, 1)))
     along = total_of(jnp.sum(residual * change, axis=0, keepdims=True))
     square = total_of(jnp.sum(change * change, axis=0, keepdims=True))
     share(along, square, lsend, lbuf, 10)
@@ -594,22 +630,28 @@
 def solution(mesh):
     shape = tuple(mesh.shape[name] for name in ("band", "dx", "dy"))
     nb, nx, ny = shape
-    held = constants()
+    table, packed_constants = packed()
 
     def on_device(wave_bands, potential, atom_offsets, proj_counts, dh_matrix, ds_matrix):
         vmem = pl.BlockSpec(memory_space=pltpu.VMEM)
         smem = pl.BlockSpec(memory_space=pltpu.SMEM)
         v = lambda *dims: pltpu.VMEM(dims, F32)
         bands, resid, energy = pl.pallas_call(
-            functools.partial(kernel, shape),
+            functools.partial(kernel, shape, table),
             out_shape=(
                 jax.ShapeDtypeStruct((128, 128), F32),
                 jax.ShapeDtypeStruct((128, 128), F32),
                 jax.ShapeDtypeStruct((1,), F32),
             ),
-            in_specs=[vmem, vmem, smem, smem, vmem, vmem] + [vmem] * len(NAMES),
+            in_specs=[pl.BlockSpec(memory_space=pltpu.HBM)] * 7,
             out_specs=(vmem, vmem, smem),
             scratch_shapes=[
+                v(128, 128),
+                v(128, 32),
+                pltpu.SMEM((1, 3, 1, ATOMS), jnp.int32),
+                pltpu.SMEM((1, 1, ATOMS), jnp.int32),
+                v(2, 9, ATOMS, 9),
+                pltpu.VMEM(packed_constants.shape, BF16),
                 v(96, 128),
                 v(144, 128),
                 v(144, 128),
@@ -619,9 +661,9 @@
                 v(2, 128, 128),
                 v(nb, 128, 128),
                 v(8, 128),
-                v(24, 8, 128),
+                v(14, 8, 128),
                 v(8, 128),
-                v(24, 8, 128),
+                v(14, 8, 128),
                 v(2, 128, 128),
                 v(2, 16, 128),
                 v(2, 48, 128),
@@ -633,22 +675,24 @@
                 v(nx * ny, 1, 128),
                 v(1, 128),
                 v(nx * ny, 1, 128),
-                v(4, 128, 128),
+                pltpu.VMEM((2, 128, 512), BF16),
+                pltpu.VMEM((2, 512, 128), BF16),
                 v(5, 128, 128),
+                pltpu.SemaphoreType.DMA((7,)),
                 pltpu.SemaphoreType.DMA((11,)),
                 pltpu.SemaphoreType.DMA((11,)),
             ],
             compiler_params=pltpu.CompilerParams(
-                collective_id=0, has_side_effects=True, vmem_limit_bytes=40 << 20
+                collective_id=0, has_side_effects=True, vmem_limit_bytes=60 << 20
             ),
         )(
             wave_bands.reshape(128, 128),
             potential.reshape(128, 32),
-            atom_offsets,
+            jnp.transpose(atom_offsets, (0, 3, 1, 2)),
             proj_counts,
-            dh_matrix.reshape(ATOMS, 9, 9),
-            ds_matrix.reshape(ATOMS, 9, 9),
-            *[held[name] for name in NAMES],
+            jnp.transpose(dh_matrix, (0, 1, 3, 2, 4)).reshape(9, ATOMS, 9),
+            jnp.transpose(ds_matrix, (0, 1, 3, 2, 4)).reshape(9, ATOMS, 9),
+            jnp.asarray(packed_constants),
         )
         return bands.reshape(1, CX, CY, NZ), resid.reshape(1, CX, CY, NZ), energy
 

time: 66.1 us -> 44.3 us (0.67)
  local copies, waits for them, and re-layouts: 17.6 us -> 2.95 us
  Pallas kernels: 45.3 us -> 38.7 us
    unnamed x39 -> x2, local copies, waits for them, and re-layouts: 16.9 us -> 2.95 us
    pallas_call x1, Pallas kernels: 45.3 us -> 38.7 us  [on_device(): pl.pallas_call(functools.partial(kernel, shape, table), out_shape=(jax.Sh...]
    reshape x1 -> x0, local copies, waits for them, and re-layouts: 0.75 us -> none  [on_device(): ds_matrix.reshape(ATOMS, 9, 9)]
where the time goes in v1:
time: 44.3 us; the launch traced here: 44.1 us
  Pallas kernels  38.7 us (87%)
  local copies, waits for them, and re-layouts  2.95 us (7%)
  between operations  2.45 us (6%)
    pallas_call x1, Pallas kernels, on_device(): pl.pallas_call(functools.partial(kernel, shape, table), out_shape=(jax.Sh...  38.7 us
    unnamed x2, local copies, waits for them, and re-layouts  2.95 us

profile of v1, /device:TPU:1, one launch (start us, length us, event | category | flops | bytes accessed | tf_op | source)
XLA Modules:
  0.0 44.1 jit_solution(1144956126210583996)
XLA Ops:
  0.6 38.7 %shard_map.94 = (f32[128,128]{1,0:T(8,128)}, f32[128,128]{1,0:T(8,128)}, f32[1]{0:T(128)}) custom-call(f32[128,128]{1,0:T(8,128)} %bitcast.11, f32[128,32]{1,0:T(8,128)} %bitcast.12, s32[1,3,1,4]{3,2,1,0:T(1,128)} %bitcast.17, s32[1,1,4]{2,1,0:T(1,128)} %refs_3_.1, f32[9,4,9]{2,1,0:T(4,128)} %bitcast.15, f32[9,4,9]{2,1,0:T(4,128)} %bitcast.16, ...), custom_call_target="tpu_custom_call" | custom-call | tf_op jit(solution)/shard_map/pallas_call | solution.py:639
  39.3 1.5 %copy.13 = f32[1,8,16,128]{3,2,1,0:T(8,128)} copy(f32[1,8,16,128]{3,2,1,0:T(8,128)} %bitcast.14) | data formatting | bytes 131072
  40.8 1.5 %copy.14 = f32[1,8,16,128]{3,2,1,0:T(8,128)} copy(f32[1,8,16,128]{3,2,1,0:T(8,128)} %bitcast.13) | data formatting | bytes 131072

commit v2 on v1

--- a/solution.py
+++ b/solution.py
@@ -101,7 +101,9 @@
 
 NEAR = [(a, b) for a in (-1, 0, 1) for b in (-1, 0, 1) if (a, b) != (0, 0)]
 FAR = [(a, b) for a in (-2, -1, 0, 1, 2) for b in (-1, 0, 1) if (a, b) != (0, 0)]
-GREET = [(a, b) for a in (-1, 0, 1) for b in (-2, -1, 0, 1, 2) if (a, b) != (0, 0)]
+GREET = NEAR + [(-1, -2), (1, -2)]
+WINDOWS = [(a, b) for a in (0, 3, 6) for b in range(8) if (a, b) != (0, 0)]
+SIDES = [(-1, 0), (1, 0)]
 
 
 def blocks(own, wide, step, targets):
@@ -291,11 +293,11 @@
     nb, nx, ny = shape
     (
         w_in, pot_in, offs_in, cnt_in, dh_in, ds_in, const_in,
-        bands_ref, resid_ref, energy_ref,
+        dirs_out, resid_out, change_out, sums_ref,
         w_ref, pot_ref, offs_ref, cnt_ref, d_ref, const,
-        stage, halo, halo2, dirs, info, infos, infot, pots, qbuf, qrecv, qbuf2, qrecv2,
-        fields, bface, bhalo, one_s, one_r, two_s, two_r, esend, ebuf, lsend, lbuf, zfun, zturn, wfun,
-        lsem, ssem, rsem,
+        stage, halo, halo2, dirs, resid, changes, geo, geos, info, infos, infot, pots, qbuf, qrecv, qbuf2, qrecv2,
+        fields, bface, bhalo, one_s, one_r, two_s, two_r, esend, ebuf, nbuf, nrecv, lsend, lbuf, zfun, zturn, wfun,
+        lsem, ssem, rsem, osem,
     ) = refs
     loads = [
         pltpu.make_async_copy(src, dst, lsem.at[n])
@@ -342,7 +344,15 @@
     me = ix * ny + iy
     slot = lax.rem(ix, 4) * 4 + lax.rem(iy, 4)
 
+    def kept(n):
+        src, dst = ((dirs, dirs_out), (resid, resid_out), (changes, change_out))[n]
+        return pltpu.make_async_copy(src, dst, osem.at[n])
+
+    def keep(n):
+        kept(n).start()
+
     infos[...] = jnp.zeros_like(infos)
+    geos[...] = jnp.zeros_like(geos)
     barrier = pltpu.get_barrier_semaphore()
 
     for a, b in GREET:
@@ -350,32 +360,40 @@
     for i in range(1, nb):
         pl.semaphore_signal(barrier, inc=1, device_id=device(0, 0, i), device_id_type=MESH)
 
-    for load in loads[:6]:
-        load.wait()
+    lane = lax.broadcasted_iota(jnp.int32, (1, 128), 1)
+    lane8 = lax.broadcasted_iota(jnp.int32, (8, 128), 1)
+    row8 = lax.broadcasted_iota(jnp.int32, (8, 128), 0)
+    loads[0].wait()
+    loads[1].wait()
+    centres = jnp.zeros((8, 128), F32)
+    for k in range(ATOMS):
+        for m, v in enumerate((offs_ref[0, 0, 0, k], offs_ref[0, 1, 0, k], offs_ref[0, 2, 0, k], cnt_ref[0, 0, k])):
+            centres = jnp.where((lax.rem(row8, 4) == k) & (lane8 == m), v.astype(F32), centres)
+    geo[...] = centres
+    geos[slot] = centres
+    loads[4].wait()
     for j in range(3):
         stage[8 * j : 8 * j + 8, :] = w_ref[pl.ds(j, 8, stride=16), :]
         stage[24 + 8 * j : 32 + 8 * j, :] = w_ref[pl.ds(13 + j, 8, stride=16), :]
-    row = lax.broadcasted_iota(jnp.int32, (128, 128), 0)
-    lane = lax.broadcasted_iota(jnp.int32, (1, 128), 1)
-    place = (lax.broadcasted_iota(jnp.int32, (32, 128), 0) + 32 * ib == lax.broadcasted_iota(jnp.int32, (32, 128), 1)).astype(F32)
-    place = place.astype(BF16)
-    high, low = split(pot_ref[...])
-    rest = pot_ref[...] - high.astype(F32) - low.astype(F32)
-    pots[ib] = dot(high, place) + dot(low, place) + dot(rest.astype(BF16), place)
+
+    pl.semaphore_wait(barrier, len(GREET) + nb - 1)
+
+    for a, b in NEAR:
+        send(geo, geos.at[slot], 11, device(a, b))
+    send(w_ref.at[pl.ds(0, 48)], halo.at[pl.ds(48, 48)], 1, device(-1, 0))
+    send(w_ref.at[pl.ds(80, 48)], halo.at[pl.ds(0, 48)], 1, device(1, 0))
+    send(stage.at[pl.ds(0, 24)], halo.at[pl.ds(120, 24)], 1, device(0, -1))
+    send(stage.at[pl.ds(24, 24)], halo.at[pl.ds(96, 24)], 1, device(0, 1))
+    for load in (loads[2], loads[3], loads[5]):
+        load.wait()
     crossed, p_from, p_to = lane // 40, (lane // 8) % 5, lane % 8
-    lane4 = lax.broadcasted_iota(jnp.int32, (ATOMS, 128), 1)
-    atom4 = lax.broadcasted_iota(jnp.int32, (ATOMS, 128), 0)
     for right in (0, 1):
         j_of = projector_of(p_from, (crossed != right))
         i_of = projector_of(p_to, lane * 0 + right == 1)
         chosen = [((i_of == i) & (lane < 80)).astype(F32) for i in range(9)]
         from_j = [(j_of == j).astype(F32) for j in range(9)]
-        place_of = jnp.zeros((ATOMS, 128), F32)
-        for k in range(ATOMS):
-            for m, v in enumerate((offs_ref[0, 0, 0, k], offs_ref[0, 1, 0, k], offs_ref[0, 2, 0, k], cnt_ref[0, 0, k])):
-                place_of = jnp.where((atom4 == k) & (lane4 == 80 + m), v.astype(F32), place_of)
         for n in range(2):
-            rows = place_of if n == 0 else jnp.zeros((ATOMS, 128), F32)
+            rows = jnp.zeros((ATOMS, 128), F32)
             for i in range(9):
                 of_i = d_ref[n, i]
                 full = of_i[:, 0:1] * from_j[0]
@@ -384,34 +402,30 @@
                 rows = rows + full * chosen[i]
             info[4 * right : 4 * right + 4, 128 * n : 128 * n + 128] = rows
     infos[slot] = info[...]
-
-    pl.semaphore_wait(barrier, len(GREET) + nb - 1)
-
     for a, b in NEAR:
         send(info, infos.at[slot], 0, device(a, b))
-    send(w_ref.at[pl.ds(0, 48)], halo.at[pl.ds(48, 48)], 1, device(-1, 0))
-    send(w_ref.at[pl.ds(80, 48)], halo.at[pl.ds(0, 48)], 1, device(1, 0))
-    send(stage.at[pl.ds(0, 24)], halo.at[pl.ds(120, 24)], 1, device(0, -1))
-    send(stage.at[pl.ds(24, 24)], halo.at[pl.ds(96, 24)], 1, device(0, 1))
+    place = (
+        lax.broadcasted_iota(jnp.int32, (32, 128), 0) + 32 * ib == lax.broadcasted_iota(jnp.int32, (32, 128), 1)
+    ).astype(BF16)
+    high, low = split(pot_ref[...])
+    rest = pot_ref[...] - high.astype(F32) - low.astype(F32)
+    pots[ib] = dot(high, place) + dot(low, place) + dot(rest.astype(BF16), place)
     for i in range(1, nb):
         send(pots.at[ib], pots.at[ib], 2, device(0, 0, i))
     w = w_ref[...]
     loads[6].wait()
     kin = from_left("kin_own", w) + from_right(w, "kin_z")
 
-    arrive(infos.at[pl.ds(0, 8)], 0)
-    for n in range(2):
-        infot[n] = jnp.swapaxes(infos[:, :, 128 * n : 128 * n + 128].reshape(128, 128), 0, 1)
+    arrive(geos.at[pl.ds(0, 8)], 11)
+    centres = jnp.swapaxes(geos[...].reshape(128, 128), 0, 1)
     slot_x, slot_y = lane // 32, (lane // 8) % 4
     right_lane = (lane // 4) % 2 == 1
     rel_x = lax.rem(slot_x - ix + 1 + 16, 4) - 1
     rel_y = lax.rem(slot_y - iy + 1 + 16, 4) - 1
-    own_lane = ((rel_x == 0) & (rel_y == 0)).astype(F32)
-    centre_x = infot[0, 80:81, :] + (rel_x * CX).astype(F32)
-    centre_y = infot[0, 81:82, :] + (rel_y * CY).astype(F32)
-    centre_z = infot[0, 82:83, :]
-    count = infot[0, 83:84, :]
-    row8 = lax.broadcasted_iota(jnp.int32, (8, 128), 0)
+    centre_x = centres[0:1, :] + (rel_x * CX).astype(F32)
+    centre_y = centres[1:2, :] + (rel_y * CY).astype(F32)
+    centre_z = centres[2:3, :]
+    count = centres[3:4, :]
     active = (projector_of(row8, jnp.broadcast_to(right_lane, (8, 128))).astype(F32) < count).astype(F32)
 
     def bells(n, centre):
@@ -444,12 +458,12 @@
     ).reshape(128, 128)
     tile_of = (0, 1, 1, 2, 3)
 
-    def overlaps(field):
+    def overlaps(field, more):
         part = dot3(split(field), (zfun[0], zfun[1]))
         rows = [
             jnp.sum(part[:, 128 * tile_of[p] : 128 * tile_of[p] + 128] * wfun[p], axis=0, keepdims=True) for p in range(5)
         ]
-        return jnp.concatenate(rows + [jnp.zeros((3, 128), F32)], axis=0)
+        return jnp.concatenate(rows + more + [jnp.zeros((3 - len(more), 128), F32)], axis=0)
 
     keep_x = {-2: (rel_x == -1).astype(F32), 2: (rel_x == 1).astype(F32)}
 
@@ -489,11 +503,14 @@
         for a, b in FAR:
             send(src, dst.at[FAR.index((-a, -b))], k, device(a, b))
 
-    q_own = overlaps(w)
+    q_own = overlaps(w, [])
     qbuf[...] = q_own
     ring_send(qbuf, qrecv, 3)
     for n, v in enumerate(split(jnp.concatenate([jnp.swapaxes(z, 0, 1) for z in zs], axis=0))):
         zturn[n] = v
+    arrive(infos.at[pl.ds(0, 8)], 0)
+    for n in range(2):
+        infot[n] = jnp.swapaxes(infos[:, :, 128 * n : 128 * n + 128].reshape(128, 128), 0, 1)
 
     arrive(halo, 1)
     kin = kin + from_left("kin_side", halo[...])
@@ -503,8 +520,15 @@
     for i in range(1, nb):
         potential = potential + pots[i]
     h_local = kin + potential * w
-    num_local = jnp.sum(w * h_local, axis=0, keepdims=True)
-    den_local = jnp.sum(w * w, axis=0, keepdims=True)
+    local = jnp.concatenate(
+        [
+            jnp.sum(w * h_local, axis=0, keepdims=True), jnp.sum(w * w, axis=0, keepdims=True), jnp.zeros((6, 128), F32),
+        ],
+        axis=0,
+    )
+    nbuf[...] = local
+    for a, b in SIDES:
+        send(nbuf, nrecv.at[SIDES.index((-a, -b))], 12, device(a, b))
 
     arrive(qrecv, 3)
     q = gather_overlaps(q_own, qrecv)
@@ -512,24 +536,6 @@
 
     def total_of(v):
         return jnp.sum(v, axis=1, keepdims=True)
-
-    num = total_of(num_local + jnp.sum(q * coef_h, axis=0, keepdims=True) * own_lane)
-    den = total_of(den_local + jnp.sum(q * coef_s, axis=0, keepdims=True) * own_lane)
-
-    def share(first, second, mine, table, k):
-        mine[...] = jnp.where(lane < 64, first, second)
-        table[me] = mine[...]
-
-        def one(i, carry):
-            send(mine, table.at[me], k, device(i // ny, lax.rem(i, ny)))
-            return carry
-
-        lax.fori_loop(1, nx * ny, one, 0)
-
-    def shared(table, k):
-        arrive(table.at[pl.ds(0, nx * ny - 1)], k)
-        total = jnp.sum(table[...], axis=0)
-        return total[:, 0:1], total[:, 64:65]
 
     both_terms = correction(jnp.concatenate([weights(coef_h), weights(coef_s)], axis=0))
     h_w = h_local + both_terms[:128]
@@ -537,13 +543,32 @@
     fields[0] = h_w
     fields[1] = s_w
 
-    for f in range(2):
-        bface[f, 0:8, :] = fields[f, pl.ds(0, 8, stride=16), :]
-        bface[f, 8:16, :] = fields[f, pl.ds(15, 8, stride=16), :]
-    send(fields.at[:, pl.ds(0, 16)], bhalo.at[:, pl.ds(16, 16)], 5, device(-1, 0))
-    send(fields.at[:, pl.ds(112, 16)], bhalo.at[:, pl.ds(0, 16)], 5, device(1, 0))
-    send(bface.at[:, pl.ds(0, 8)], bhalo.at[:, pl.ds(40, 8)], 5, device(0, -1))
-    send(bface.at[:, pl.ds(8, 8)], bhalo.at[:, pl.ds(32, 8)], 5, device(0, 1))
+    of_atoms = jnp.concatenate(
+        [
+            jnp.sum(q * coef_h, axis=0, keepdims=True), jnp.sum(q * coef_s, axis=0, keepdims=True), jnp.zeros((6, 128), F32),
+        ],
+        axis=0,
+    )
+    arrive(nrecv, 12)
+
+    near = of_atoms * (rel_y == 0).astype(F32)
+    esend[1] = near * (rel_x <= 0).astype(F32) + local + nrecv[0]
+    esend[0] = near * (rel_x <= 1).astype(F32) + local + nrecv[0] + nrecv[1]
+
+    def share(first, second, mine, table, k):
+        mine[...] = jnp.where(lane < 64, first, second)
+        table[me] = mine[...]
+
+        for a in range(nx):
+            for b in range(ny):
+                if (a, b) != (0, 0):
+                    send(mine, table.at[me], k, device(a, b))
+
+    def shared(table, k):
+        arrive(table.at[pl.ds(0, nx * ny - 1)], k)
+        total = jnp.sum(table[...], axis=0)
+        return total[:, 0:1], total[:, 64:65]
+
     flat = from_right(jnp.concatenate([h_w, s_w], axis=1), "down_z")
     one = from_left("down_one", jnp.concatenate([flat[:, :128], flat[:, 128:256]], axis=0))
     one_s[...] = one[:ROWS_ONE]
@@ -564,7 +589,15 @@
         n = pad8(len(block))
         send(two_s.at[pl.ds(at, n)], two_r.at[pl.ds(at, n)], 7, device(*t))
 
-    share(num, den, esend, ebuf, 4)
+    for n, (a, b) in enumerate(WINDOWS):
+        send(esend.at[a // 6], ebuf.at[n], 4, device(-a, -b))
+    for f in range(2):
+        bface[f, 0:8, :] = fields[f, pl.ds(0, 8, stride=16), :]
+        bface[f, 8:16, :] = fields[f, pl.ds(15, 8, stride=16), :]
+    send(fields.at[:, pl.ds(0, 16)], bhalo.at[:, pl.ds(16, 16)], 5, device(-1, 0))
+    send(fields.at[:, pl.ds(112, 16)], bhalo.at[:, pl.ds(0, 16)], 5, device(1, 0))
+    send(bface.at[:, pl.ds(0, 8)], bhalo.at[:, pl.ds(40, 8)], 5, device(0, -1))
+    send(bface.at[:, pl.ds(8, 8)], bhalo.at[:, pl.ds(32, 8)], 5, device(0, 1))
 
     arrive(one_s, 6)
     level1 = one_r[...]
@@ -574,9 +607,12 @@
     x2 = from_left("sweep_two", jnp.concatenate([flat[:, :128], flat[:, 128:256], flat[:, 256:]], axis=0))
     flat = from_right(x2, "up_one_z")
     x1 = from_left("up_one", jnp.concatenate([level1, level1_z, flat[:, :128], flat[:, 128:]], axis=0))
-    num, den = shared(ebuf, 4)
-    energy = num / den
+    arrive(ebuf, 4)
+    sums = jnp.sum(ebuf[...], axis=0) + esend[0]
+    energy = total_of(sums[0:1]) / total_of(sums[1:2])
     residual = h_w - energy * s_w
+    resid[...] = residual
+    keep(1)
     x1 = x1 - energy * pltpu.roll(x1, 64, 1)
     flat = from_right(x1, "up_zero_z")
     arrive(bhalo, 5)
@@ -593,9 +629,10 @@
     send(dirs.at[pl.ds(80, 48)], halo2.at[pl.ds(0, 48)], 8, device(1, 0))
     send(stage.at[pl.ds(48, 24)], halo2.at[pl.ds(120, 24)], 8, device(0, -1))
     send(stage.at[pl.ds(72, 24)], halo2.at[pl.ds(96, 24)], 8, device(0, 1))
-    q_own = overlaps(direction)
+    q_own = overlaps(direction, [])
     qbuf2[...] = q_own
     ring_send(qbuf2, qrecv2, 9)
+    keep(0)
     change = from_left("kin_own", direction) + from_right(direction, "kin_z")
     change = change + (potential - energy) * direction
     arrive(halo2, 8)
@@ -606,13 +643,17 @@
     along = total_of(jnp.sum(residual * change, axis=0, keepdims=True))
     square = total_of(jnp.sum(change * change, axis=0, keepdims=True))
     share(along, square, lsend, lbuf, 10)
+    changes[...] = change
+    keep(2)
 
     left(infos.at[pl.ds(0, 8)], 0)
     left(halo, 1)
     if nb > 1:
         left(pots.at[pl.ds(0, nb - 1)], 2)
     left(qrecv, 3)
-    left(ebuf.at[pl.ds(0, nx * ny - 1)], 4)
+    left(ebuf, 4)
+    left(geos.at[pl.ds(0, 8)], 11)
+    left(nrecv, 12)
     left(bhalo, 5)
     left(one_s, 6)
     left(two_s, 7)
@@ -621,10 +662,16 @@
     left(lbuf.at[pl.ds(0, nx * ny - 1)], 10)
 
     along, square = shared(lbuf, 10)
-    step = -along / square
-    bands_ref[...] = w + step * direction
-    resid_ref[...] = residual + step * change
-    energy_ref[0] = energy[0, 0]
+    sums_ref[...] = jnp.where(lane < 64, -along / square, energy)
+    for n in range(3):
+        kept(n).wait()
+
+
+def finish(w_ref, dirs_ref, resid_ref, change_ref, sums_ref, bands_ref, new_ref, energy_ref):
+    step = sums_ref[0:1, 0:1]
+    bands_ref[...] = w_ref[...] + step * dirs_ref[...]
+    new_ref[...] = resid_ref[...] + step * change_ref[...]
+    energy_ref[0] = sums_ref[0, 127]
 
 
 def solution(mesh):
@@ -636,15 +683,13 @@
         vmem = pl.BlockSpec(memory_space=pltpu.VMEM)
         smem = pl.BlockSpec(memory_space=pltpu.SMEM)
         v = lambda *dims: pltpu.VMEM(dims, F32)
-        bands, resid, energy = pl.pallas_call(
+        hbm = pl.BlockSpec(memory_space=pltpu.HBM)
+        grid = jax.ShapeDtypeStruct((128, 128), F32)
+        dirs, resid, changes, sums = pl.pallas_call(
             functools.partial(kernel, shape, table),
-            out_shape=(
-                jax.ShapeDtypeStruct((128, 128), F32),
-                jax.ShapeDtypeStruct((128, 128), F32),
-                jax.ShapeDtypeStruct((1,), F32),
-            ),
-            in_specs=[pl.BlockSpec(memory_space=pltpu.HBM)] * 7,
-            out_specs=(vmem, vmem, smem),
+            out_shape=(grid, grid, grid, jax.ShapeDtypeStruct((1, 128), F32)),
+            in_specs=[hbm] * 7,
+            out_specs=(hbm, hbm, hbm, vmem),
             scratch_shapes=[
                 v(128, 128),
                 v(128, 32),
@@ -656,6 +701,10 @@
                 v(144, 128),
                 v(144, 128),
                 v(128, 128),
+                v(128, 128),
+                v(128, 128),
+                v(8, 128),
+                v(16, 8, 128),
                 v(8, 256),
                 v(16, 8, 256),
                 v(2, 128, 128),
@@ -671,16 +720,19 @@
                 v(STACK_ONE, 128),
                 v(ROWS_TWO, 128),
                 v(STACK_TWO, 128),
-                v(1, 128),
-                v(nx * ny, 1, 128),
+                v(2, 8, 128),
+                v(23, 8, 128),
+                v(8, 128),
+                v(2, 8, 128),
                 v(1, 128),
                 v(nx * ny, 1, 128),
                 pltpu.VMEM((2, 128, 512), BF16),
                 pltpu.VMEM((2, 512, 128), BF16),
                 v(5, 128, 128),
                 pltpu.SemaphoreType.DMA((7,)),
-                pltpu.SemaphoreType.DMA((11,)),
-                pltpu.SemaphoreType.DMA((11,)),
+                pltpu.SemaphoreType.DMA((13,)),
+                pltpu.SemaphoreType.DMA((13,)),
+                pltpu.SemaphoreType.DMA((3,)),
             ],
             compiler_params=pltpu.CompilerParams(
                 collective_id=0, has_side_effects=True, vmem_limit_bytes=60 << 20
@@ -694,6 +746,13 @@
             jnp.transpose(ds_matrix, (0, 1, 3, 2, 4)).reshape(9, ATOMS, 9),
             jnp.asarray(packed_constants),
         )
+        bands, resid, energy = pl.pallas_call(
+            finish,
+            out_shape=(grid, grid, jax.ShapeDtypeStruct((1,), F32)),
+            in_specs=[vmem] * 5,
+            out_specs=(vmem, vmem, smem),
+            compiler_params=pltpu.CompilerParams(vmem_limit_bytes=60 << 20),
+        )(wave_bands.reshape(128, 128), dirs, resid, changes, sums)
         return bands.reshape(1, CX, CY, NZ), resid.reshape(1, CX, CY, NZ), energy
 
     return jax.shard_map(

time: 44.3 us -> 41.8 us (0.944)
  local copies, waits for them, and re-layouts: 2.95 us -> 0 us
  Pallas kernels: 38.7 us -> 41 us
  between operations: 2.45 us -> 0.64 us
    unnamed x2 -> x0, local copies, waits for them, and re-layouts: 2.95 us -> none
    pallas_call x1 -> x2, Pallas kernels: 38.7 us -> 41 us  [the longest x1 39.3 us: on_device(): pl.pallas_call(functools.partial(kernel, shape, table), out_shape=(grid,...]
where the time goes in v2:
time: 41.8 us; the launch traced here: 41.6 us
  Pallas kernels  41 us (98%)
  between operations  0.64 us (2%)
    pallas_call x1, Pallas kernels, on_device(): pl.pallas_call(functools.partial(kernel, shape, table), out_shape=(grid,...  39.3 us
    pallas_call x1, Pallas kernels, on_device(): pl.pallas_call(finish, out_shape=(grid, grid, jax.ShapeDtypeStruct((1,),...  1.68 us

profile of v2, /device:TPU:1, one launch (start us, length us, event | category | flops | bytes accessed | tf_op | source)
XLA Modules:
  0.0 41.6 jit_solution(613721072974309237)
XLA Ops:
  0.6 39.3 %shard_map.94 = (f32[128,128]{1,0:T(8,128)}, f32[128,128]{1,0:T(8,128)}, f32[128,128]{1,0:T(8,128)}, f32[1,128]{1,0:T(1,128)}) custom-call(f32[128,128]{1,0:T(8,128)} %bitcast.11, f32[128,32]{1,0:T(8,128)} %bitcast.13, s32[1,3,1,4]{3,2,1,0:T(1,128)} %bitcast.16, s32[1,1,4]{2,1,0:T(1,128)} %refs_3_.1, f32[9,4,9]{2,1,0:T(4,128)} %bitcast.14, ...), custom_call_target="tpu_custom_call" | custom-call | tf_op jit(solution)/shard_map/pallas_call | solution.py:688
  39.9 1.7 %shard_map.95 = (f32[128,128]{1,0:T(8,128)}, f32[128,128]{1,0:T(8,128)}, f32[1]{0:T(128)}) custom-call(f32[128,128]{1,0:T(8,128)} %bitcast.12, f32[128,128]{1,0:T(8,128)} %get-tuple-element.10.dirs_ref, f32[128,128]{1,0:T(8,128)} %get-tuple-element.11.resid_ref, f32[128,128]{1,0:T(8,128)} %get-tuple-element.12.change_ref, f32[1,128]{1,0:T(1,128)} %get-tuple-element.13.sums_ref), custom_call_target="tpu_custom_call" | custom-call | tf_op jit(solution)/shard_map/pallas_call | solution.py:749

commit v3 on v2

--- a/solution.py
+++ b/solution.py
@@ -106,38 +106,59 @@
 SIDES = [(-1, 0), (1, 0)]
 
 
-def blocks(own, wide, step, targets):
+def within(among, of, reach):
+    return [c for c in among if min(abs(c[0] - d[0]) + abs(c[1] - d[1]) for d in of) <= reach]
+
+
+ONE_USED = [c for c in ONE if not (c[0] in (-1, 4) and c[1] in (-1, 8))]
+
+
+def blocks(own, wide, step, targets, halves):
     wide = set(wide)
     table, at = {}, 0
     for t in targets:
         block = [c for c in own if (c[0] - step[0] * t[0], c[1] - step[1] * t[1]) in wide]
-        table[t] = (at, block)
-        at += pad8(len(block))
+        rows = pad8((len(block) + halves - 1) // halves)
+        table[t] = (at, rows, block)
+        at += rows
     return table, at
 
 
-BLOCKS_ONE, ROWS_ONE = blocks(ONE, ONE_WIDE, (4, 8), NEAR)
-BLOCKS_TWO, ROWS_TWO = blocks(TWO, TWO_WIDE, (2, 4), FAR)
+BLOCKS_ONE, ROWS_ONE = blocks(ONE_USED, within(ONE_WIDE, ONE_USED, 1), (4, 8), NEAR, 1)
+BLOCKS_TWO, ROWS_TWO = blocks(TWO, within(TWO_WIDE, TWO, 2), (2, 4), FAR, 2)
+MIXED, ROWS_NEAR, ROWS_FAR = {}, 0, 0
+for tile in FAR:
+    rows_one = BLOCKS_ONE[tile][1] if tile in BLOCKS_ONE else 0
+    rows_two = BLOCKS_TWO[tile][1]
+    if rows_one:
+        MIXED[tile] = (ROWS_NEAR, rows_one, rows_two)
+        ROWS_NEAR += rows_one + rows_two
+    else:
+        MIXED[tile] = (ROWS_FAR, 0, rows_two)
+        ROWS_FAR += rows_two
 OWN_ONE = pad8(len(ONE))
 OWN_TWO = 32
 STACK_ONE = ROWS_ONE + OWN_ONE
 STACK_TWO = ROWS_TWO + OWN_TWO
 
 
-def senders(table, rows, own):
-    m = np.zeros((rows + (OWN_ONE if own is ONE else OWN_TWO), len(own)))
-    for at, block in table.values():
-        m[at : at + len(block)] = pick(block, own)
-    m[rows : rows + len(own)] = np.eye(len(own))
+def senders(table, rows, own, own_rows, half=0):
+    m = np.zeros((rows + own_rows, len(own)))
+    for at, n, block in table.values():
+        part = block[half * n : half * n + n]
+        m[at : at + len(part)] = pick(part, own)
+    if half == 0:
+        m[rows : rows + len(own)] = np.eye(len(own))
     return m
 
 
-def receivers(table, rows, own, wide, step):
-    m = np.zeros((len(wide), rows + (OWN_ONE if own is ONE else OWN_TWO)))
-    for t, (at, block) in table.items():
-        here = [(i - step[0] * t[0], j - step[1] * t[1]) for i, j in block]
-        m[:, at : at + len(block)] = pick(wide, here)
-    m[:, rows : rows + len(own)] = pick(wide, own)
+def receivers(table, rows, own, own_rows, wide, step, half=0):
+    m = np.zeros((len(wide), rows + own_rows))
+    for t, (at, n, block) in table.items():
+        here = [(i - step[0] * t[0], j - step[1] * t[1]) for i, j in block[half * n : half * n + n]]
+        m[:, at : at + len(here)] = pick(wide, here)
+    if half == 0:
+        m[:, rows : rows + len(own)] = pick(wide, own)
     return m
 
 
@@ -171,23 +192,23 @@
     avg = average(ONE, ring0)
     one_plane = avg @ (pick(ring0, FINE) / 3.0 + SIDE[0] * cross(ring0, FINE))
     one_along = avg @ pick(ring0, FINE) * SIDE[0]
-    send = senders(BLOCKS_ONE, ROWS_ONE, ONE)
+    send = senders(BLOCKS_ONE, ROWS_ONE, ONE, OWN_ONE)
     c["down_one"] = np.concatenate([send @ one_plane, send @ one_along], axis=1)
 
     ring1 = cells(-2, 6, -2, 10)
     avg = average(TWO, ring1)
     two_plane = avg @ (pick(ring1, ONE) / 3.0 + SIDE[1] * cross(ring1, ONE))
     two_along = avg @ pick(ring1, ONE) * SIDE[1]
-    send = senders(BLOCKS_TWO, ROWS_TWO, TWO)
+    sends = [senders(BLOCKS_TWO, ROWS_TWO, TWO, OWN_TWO, half) for half in (0, 1)]
     c["down_two"] = np.concatenate(
-        [send @ two @ one for two in (two_plane, two_along) for one in (one_plane, one_along)], axis=1
+        [send @ two @ one for send in sends for two in (two_plane, two_along) for one in (one_plane, one_along)], axis=1
     )
     h0, n0, h1, n1 = halve_z(NZ), along_z(NZ), halve_z(64), along_z(64)
     c["down_z"] = np.concatenate(
         [both(m) for m in (h0, n0 @ h0, h0 @ h1, n0 @ h0 @ h1, h0 @ n1 @ h1, n0 @ h0 @ n1 @ h1)], axis=1
     )
 
-    take = receivers(BLOCKS_TWO, ROWS_TWO, TWO, TWO_WIDE, (2, 4))
+    takes = [receivers(BLOCKS_TWO, ROWS_TWO, TWO, OWN_TWO, TWO_WIDE, (2, 4), half) for half in (0, 1)]
     mid = cells(-2, 4, -2, 6)
     n1 = cross(TWO, TWO_WIDE)
     n2 = cross(TWO, mid) @ cross(mid, TWO_WIDE)
@@ -198,13 +219,15 @@
         g * (5.0 / 3.0 * k * here + 2.0 * k * k * n1),
         g * k * k * here,
     ]
-    c["sweep_two"] = np.concatenate([t @ take for t in terms], axis=1)
+    c["sweep_two"] = np.concatenate([t @ take for take in takes for t in terms], axis=1)
     nz = along_z(32)
+    places = [grown(both(m), 64, 128) for m in (np.eye(32), nz, nz @ nz)]
+    blank = np.zeros((64, 128))
     c["sweep_two_z"] = np.concatenate(
-        [grown(both(m), 128, 128) for m in (np.eye(32), nz, nz @ nz)], axis=1
-    )
-
-    take = receivers(BLOCKS_ONE, ROWS_ONE, ONE, ONE_WIDE, (4, 8))
+        [np.concatenate([m, blank]) for m in places] + [np.concatenate([blank, m]) for m in places], axis=1
+    )
+
+    take = receivers(BLOCKS_ONE, ROWS_ONE, ONE, OWN_ONE, ONE_WIDE, (4, 8))
     g, k = GAIN[1], SIDE[1]
     here, n1 = pick(ONE, ONE_WIDE), cross(ONE, ONE_WIDE)
     up = spread_to(ONE_WIDE, TWO)
@@ -296,7 +319,7 @@
         dirs_out, resid_out, change_out, sums_ref,
         w_ref, pot_ref, offs_ref, cnt_ref, d_ref, const,
         stage, halo, halo2, dirs, resid, changes, geo, geos, info, infos, infot, pots, qbuf, qrecv, qbuf2, qrecv2,
-        fields, bface, bhalo, one_s, one_r, two_s, two_r, esend, ebuf, nbuf, nrecv, lsend, lbuf, zfun, zturn, wfun,
+        fields, bface, bhalo, near_s, near_r, far_s, far_r, esend, ebuf, nbuf, nrecv, lsend, lbuf, zfun, zturn, wfun,
         lsem, ssem, rsem, osem,
     ) = refs
     loads = [
@@ -386,6 +409,18 @@
     send(stage.at[pl.ds(24, 24)], halo.at[pl.ds(96, 24)], 1, device(0, 1))
     for load in (loads[2], loads[3], loads[5]):
         load.wait()
+    packed_pot = jnp.zeros((32, 128), F32)
+    for g in range(4):
+        place = (
+            lax.broadcasted_iota(jnp.int32, (32, 128), 0) + 32 * g == lax.broadcasted_iota(jnp.int32, (32, 128), 1)
+        ).astype(BF16)
+        part = pot_ref[32 * g : 32 * g + 32, :]
+        high, low = split(part)
+        rest = part - high.astype(F32) - low.astype(F32)
+        packed_pot = packed_pot + dot(high, place) + dot(low, place) + dot(rest.astype(BF16), place)
+    pots[ib] = packed_pot
+    for i in range(1, nb):
+        send(pots.at[ib], pots.at[ib], 2, device(0, 0, i))
     crossed, p_from, p_to = lane // 40, (lane // 8) % 5, lane % 8
     for right in (0, 1):
         j_of = projector_of(p_from, (crossed != right))
@@ -404,14 +439,6 @@
     infos[slot] = info[...]
     for a, b in NEAR:
         send(info, infos.at[slot], 0, device(a, b))
-    place = (
-        lax.broadcasted_iota(jnp.int32, (32, 128), 0) + 32 * ib == lax.broadcasted_iota(jnp.int32, (32, 128), 1)
-    ).astype(BF16)
-    high, low = split(pot_ref[...])
-    rest = pot_ref[...] - high.astype(F32) - low.astype(F32)
-    pots[ib] = dot(high, place) + dot(low, place) + dot(rest.astype(BF16), place)
-    for i in range(1, nb):
-        send(pots.at[ib], pots.at[ib], 2, device(0, 0, i))
     w = w_ref[...]
     loads[6].wait()
     kin = from_left("kin_own", w) + from_right(w, "kin_z")
@@ -516,13 +543,19 @@
     kin = kin + from_left("kin_side", halo[...])
     if nb > 1:
         arrive(pots.at[pl.ds(0, nb - 1)], 2)
-    potential = pots[0]
-    for i in range(1, nb):
-        potential = potential + pots[i]
+    groups = []
+    for g in range(4):
+        group = jnp.zeros((32, 128), F32)
+        for i in range(nb):
+            turn = 32 * (i - g) % 128
+            part = pltpu.roll(pots[i], turn, 1) if turn else pots[i]
+            group = jnp.where(lane // 32 == i, part, group)
+        groups.append(group)
+    potential = jnp.concatenate(groups, axis=0)
     h_local = kin + potential * w
     local = jnp.concatenate(
         [
-            jnp.sum(w * h_local, axis=0, keepdims=True), jnp.sum(w * w, axis=0, keepdims=True), jnp.zeros((6, 128), F32),
+            jnp.sum(w * h_local, axis=0, keepdims=True), jnp.sum(w * w, axis=0, keepdims=True),
         ],
         axis=0,
     )
@@ -536,6 +569,20 @@
 
     def total_of(v):
         return jnp.sum(v, axis=1, keepdims=True)
+
+    of_atoms = jnp.concatenate(
+        [
+            jnp.sum(q * coef_h, axis=0, keepdims=True), jnp.sum(q * coef_s, axis=0, keepdims=True),
+        ],
+        axis=0,
+    )
+    arrive(nrecv, 12)
+
+    near = of_atoms * (rel_y == 0).astype(F32)
+    esend[1] = near * (rel_x <= 0).astype(F32) + local + nrecv[0]
+    esend[0] = near * (rel_x <= 1).astype(F32) + local + nrecv[0] + nrecv[1]
+    for n, (a, b) in enumerate(WINDOWS):
+        send(esend.at[a // 6], ebuf.at[n], 4, device(-a, -b))
 
     both_terms = correction(jnp.concatenate([weights(coef_h), weights(coef_s)], axis=0))
     h_w = h_local + both_terms[:128]
@@ -543,18 +590,6 @@
     fields[0] = h_w
     fields[1] = s_w
 
-    of_atoms = jnp.concatenate(
-        [
-            jnp.sum(q * coef_h, axis=0, keepdims=True), jnp.sum(q * coef_s, axis=0, keepdims=True), jnp.zeros((6, 128), F32),
-        ],
-        axis=0,
-    )
-    arrive(nrecv, 12)
-
-    near = of_atoms * (rel_y == 0).astype(F32)
-    esend[1] = near * (rel_x <= 0).astype(F32) + local + nrecv[0]
-    esend[0] = near * (rel_x <= 1).astype(F32) + local + nrecv[0] + nrecv[1]
-
     def share(first, second, mine, table, k):
         mine[...] = jnp.where(lane < 64, first, second)
         table[me] = mine[...]
@@ -570,27 +605,28 @@
         return total[:, 0:1], total[:, 64:65]
 
     flat = from_right(jnp.concatenate([h_w, s_w], axis=1), "down_z")
-    one = from_left("down_one", jnp.concatenate([flat[:, :128], flat[:, 128:256]], axis=0))
-    one_s[...] = one[:ROWS_ONE]
-    one_r[ROWS_ONE:STACK_ONE, :] = one[ROWS_ONE:]
-    for t in NEAR:
-        at, block = BLOCKS_ONE[t]
-        n = pad8(len(block))
-        send(one_s.at[pl.ds(at, n)], one_r.at[pl.ds(at, n)], 6, device(*t))
     lower, upper = flat[:, 256:384], flat[:, 384:]
+    turned = [lower, pltpu.roll(lower, 64, 1), upper, pltpu.roll(upper, 64, 1)]
+    on_left = lane < 64
     two = from_left(
         "down_two",
-        jnp.concatenate([lower, pltpu.roll(lower, 64, 1), upper, pltpu.roll(upper, 64, 1)], axis=0),
-    )
-    two_s[...] = two[:ROWS_TWO]
-    two_r[ROWS_TWO:STACK_TWO, :] = two[ROWS_TWO:]
+        jnp.concatenate(
+            [jnp.where(on_left, m, 0.0) for m in turned]
+            + [jnp.where(on_left, 0.0, turned[n]) for n in (1, 0, 3, 2)],
+            axis=0,
+        ),
+    )
     for t in FAR:
-        at, block = BLOCKS_TWO[t]
-        n = pad8(len(block))
-        send(two_s.at[pl.ds(at, n)], two_r.at[pl.ds(at, n)], 7, device(*t))
-
-    for n, (a, b) in enumerate(WINDOWS):
-        send(esend.at[a // 6], ebuf.at[n], 4, device(-a, -b))
+        at, n1, n2 = MIXED[t]
+        if n1 == 0:
+            far_s[at : at + n2, :] = two[BLOCKS_TWO[t][0] : BLOCKS_TWO[t][0] + n2]
+            send(far_s.at[pl.ds(at, n2)], far_r.at[pl.ds(at, n2)], 7, device(*t))
+    one = from_left("down_one", jnp.concatenate([flat[:, :128], flat[:, 128:256]], axis=0))
+    for t in NEAR:
+        at, n1, n2 = MIXED[t]
+        near_s[at : at + n1, :] = one[BLOCKS_ONE[t][0] : BLOCKS_ONE[t][0] + n1]
+        near_s[at + n1 : at + n1 + n2, :] = two[BLOCKS_TWO[t][0] : BLOCKS_TWO[t][0] + n2]
+        send(near_s.at[pl.ds(at, n1 + n2)], near_r.at[pl.ds(at, n1 + n2)], 6, device(*t))
     for f in range(2):
         bface[f, 0:8, :] = fields[f, pl.ds(0, 8, stride=16), :]
         bface[f, 8:16, :] = fields[f, pl.ds(15, 8, stride=16), :]
@@ -599,12 +635,17 @@
     send(bface.at[:, pl.ds(0, 8)], bhalo.at[:, pl.ds(40, 8)], 5, device(0, -1))
     send(bface.at[:, pl.ds(8, 8)], bhalo.at[:, pl.ds(32, 8)], 5, device(0, 1))
 
-    arrive(one_s, 6)
-    level1 = one_r[...]
+    arrive(near_s, 6)
+    level1 = jnp.concatenate(
+        [near_r[MIXED[t][0] : MIXED[t][0] + MIXED[t][1], :] for t in NEAR] + [one[ROWS_ONE:]], axis=0
+    )
     level1_z = from_right(level1, "one_z")
-    arrive(two_s, 7)
-    flat = from_right(two_r[...], "sweep_two_z")
-    x2 = from_left("sweep_two", jnp.concatenate([flat[:, :128], flat[:, 128:256], flat[:, 256:]], axis=0))
+    arrive(far_s, 7)
+    level2 = [
+        near_r[at + n1 : at + n1 + n2, :] if n1 else far_r[at : at + n2, :] for at, n1, n2 in (MIXED[t] for t in FAR)
+    ]
+    flat = from_right(jnp.concatenate(level2 + [two[ROWS_TWO:]], axis=0), "sweep_two_z")
+    x2 = from_left("sweep_two", jnp.concatenate([flat[:, 128 * n : 128 * n + 128] for n in range(6)], axis=0))
     flat = from_right(x2, "up_one_z")
     x1 = from_left("up_one", jnp.concatenate([level1, level1_z, flat[:, :128], flat[:, 128:]], axis=0))
     arrive(ebuf, 4)
@@ -655,8 +696,8 @@
     left(geos.at[pl.ds(0, 8)], 11)
     left(nrecv, 12)
     left(bhalo, 5)
-    left(one_s, 6)
-    left(two_s, 7)
+    left(near_s, 6)
+    left(far_s, 7)
     left(halo2, 8)
     left(qrecv2, 9)
     left(lbuf.at[pl.ds(0, nx * ny - 1)], 10)
@@ -708,7 +749,7 @@
                 v(8, 256),
                 v(16, 8, 256),
                 v(2, 128, 128),
-                v(nb, 128, 128),
+                v(nb, 32, 128),
                 v(8, 128),
                 v(14, 8, 128),
                 v(8, 128),
@@ -716,14 +757,14 @@
                 v(2, 128, 128),
                 v(2, 16, 128),
                 v(2, 48, 128),
-                v(ROWS_ONE, 128),
-                v(STACK_ONE, 128),
-                v(ROWS_TWO, 128),
-                v(STACK_TWO, 128),
-                v(2, 8, 128),
-                v(23, 8, 128),
-                v(8, 128),
-                v(2, 8, 128),
+                v(ROWS_NEAR, 128),
+                v(ROWS_NEAR, 128),
+                v(ROWS_FAR, 128),
+                v(ROWS_FAR, 128),
+                v(2, 2, 128),
+                v(23, 2, 128),
+                v(2, 128),
+                v(2, 2, 128),
                 v(1, 128),
                 v(nx * ny, 1, 128),
                 pltpu.VMEM((2, 128, 512), BF16),

time: 41.8 us -> 38.8 us (0.928)
  Pallas kernels: 41 us -> 38 us
    pallas_call x1, Pallas kernels: 39.3 us -> 36.3 us  [on_device(): pl.pallas_call(functools.partial(kernel, shape, table), out_shape=(grid,...]
where the time goes in v3:
time: 38.8 us; the launch traced here: 38.7 us
  Pallas kernels  38 us (98%)
  between operations  0.64 us (2%)
    pallas_call x1, Pallas kernels, on_device(): pl.pallas_call(functools.partial(kernel, shape, table), out_shape=(grid,...  36.3 us
    pallas_call x1, Pallas kernels, on_device(): pl.pallas_call(finish, out_shape=(grid, grid, jax.ShapeDtypeStruct((1,),...  1.68 us

profile of v3, /device:TPU:1, one launch (start us, length us, event | category | flops | bytes accessed | tf_op | source)
XLA Modules:
  0.0 38.7 jit_solution(17080068258991651397)
XLA Ops:
  0.6 36.3 %shard_map.94 = (f32[128,128]{1,0:T(8,128)}, f32[128,128]{1,0:T(8,128)}, f32[128,128]{1,0:T(8,128)}, f32[1,128]{1,0:T(1,128)}) custom-call(f32[128,128]{1,0:T(8,128)} %bitcast.11, f32[128,32]{1,0:T(8,128)} %bitcast.13, s32[1,3,1,4]{3,2,1,0:T(1,128)} %bitcast.16, s32[1,1,4]{2,1,0:T(1,128)} %refs_3_.1, f32[9,4,9]{2,1,0:T(4,128)} %bitcast.14, ...), custom_call_target="tpu_custom_call" | custom-call | tf_op jit(solution)/shard_map/pallas_call | solution.py:729
  37.0 1.7 %shard_map.95 = (f32[128,128]{1,0:T(8,128)}, f32[128,128]{1,0:T(8,128)}, f32[1]{0:T(128)}) custom-call(f32[128,128]{1,0:T(8,128)} %bitcast.12, f32[128,128]{1,0:T(8,128)} %get-tuple-element.10.dirs_ref, f32[128,128]{1,0:T(8,128)} %get-tuple-element.11.resid_ref, f32[128,128]{1,0:T(8,128)} %get-tuple-element.12.change_ref, f32[1,128]{1,0:T(1,128)} %get-tuple-element.13.sums_ref), custom_call_target="tpu_custom_call" | custom-call | tf_op jit(solution)/shard_map/pallas_call | solution.py:790

commit v4 on v3

--- a/solution.py
+++ b/solution.py
@@ -101,9 +101,13 @@
 
 NEAR = [(a, b) for a in (-1, 0, 1) for b in (-1, 0, 1) if (a, b) != (0, 0)]
 FAR = [(a, b) for a in (-2, -1, 0, 1, 2) for b in (-1, 0, 1) if (a, b) != (0, 0)]
-GREET = NEAR + [(-1, -2), (1, -2)]
+GREET = [(-1, -2), (1, -2), (-1, -1), (-1, 1), (1, -1), (1, 1), (-1, 0), (1, 0), (0, -1), (0, 1)]
 WINDOWS = [(a, b) for a in (0, 3, 6) for b in range(8) if (a, b) != (0, 0)]
 SIDES = [(-1, 0), (1, 0)]
+
+
+def away(tile):
+    return -(2 * min(tile[0] % 8, -tile[0] % 8) + min(tile[1] % 8, -tile[1] % 8))
 
 
 def within(among, of, reach):
@@ -316,10 +320,10 @@
     nb, nx, ny = shape
     (
         w_in, pot_in, offs_in, cnt_in, dh_in, ds_in, const_in,
-        dirs_out, resid_out, change_out, sums_ref,
+        dirs_out, resid_out, change_out, energy_out, lbuf,
         w_ref, pot_ref, offs_ref, cnt_ref, d_ref, const,
         stage, halo, halo2, dirs, resid, changes, geo, geos, info, infos, infot, pots, qbuf, qrecv, qbuf2, qrecv2,
-        fields, bface, bhalo, near_s, near_r, far_s, far_r, esend, ebuf, nbuf, nrecv, lsend, lbuf, zfun, zturn, wfun,
+        fields, bface, bhalo, near_s, near_r, far_s, far_r, esend, ebuf, nbuf, nrecv, lsend, level, zfun, zturn, wfun,
         lsem, ssem, rsem, osem,
     ) = refs
     loads = [
@@ -368,7 +372,7 @@
     slot = lax.rem(ix, 4) * 4 + lax.rem(iy, 4)
 
     def kept(n):
-        src, dst = ((dirs, dirs_out), (resid, resid_out), (changes, change_out))[n]
+        src, dst = ((dirs, dirs_out), (resid, resid_out), (changes, change_out), (level, energy_out), (lsend, lbuf.at[me]))[n]
         return pltpu.make_async_copy(src, dst, osem.at[n])
 
     def keep(n):
@@ -378,11 +382,10 @@
     geos[...] = jnp.zeros_like(geos)
     barrier = pltpu.get_barrier_semaphore()
 
+    for i in range(1, nb):
+        pl.semaphore_signal(barrier, inc=1, device_id=device(0, 0, i), device_id_type=MESH)
     for a, b in GREET:
         pl.semaphore_signal(barrier, inc=1, device_id=device(a, b), device_id_type=MESH)
-    for i in range(1, nb):
-        pl.semaphore_signal(barrier, inc=1, device_id=device(0, 0, i), device_id_type=MESH)
-
     lane = lax.broadcasted_iota(jnp.int32, (1, 128), 1)
     lane8 = lax.broadcasted_iota(jnp.int32, (8, 128), 1)
     row8 = lax.broadcasted_iota(jnp.int32, (8, 128), 0)
@@ -485,12 +488,12 @@
     ).reshape(128, 128)
     tile_of = (0, 1, 1, 2, 3)
 
-    def overlaps(field, more):
+    def overlaps(field):
         part = dot3(split(field), (zfun[0], zfun[1]))
         rows = [
             jnp.sum(part[:, 128 * tile_of[p] : 128 * tile_of[p] + 128] * wfun[p], axis=0, keepdims=True) for p in range(5)
         ]
-        return jnp.concatenate(rows + more + [jnp.zeros((3 - len(more), 128), F32)], axis=0)
+        return jnp.concatenate(rows, axis=0)
 
     keep_x = {-2: (rel_x == -1).astype(F32), 2: (rel_x == 1).astype(F32)}
 
@@ -503,7 +506,7 @@
                 line = v if line is None else line + v
             line = line * keep_x[a] if a in keep_x else line
             total = line if total is None else total + line
-        return total * active
+        return total * active[:5]
 
     def coefficients(q, n):
         swapped = jnp.where(right_lane, pltpu.roll(q, 4, 1), pltpu.roll(q, 124, 1))
@@ -527,10 +530,10 @@
         return dot3(split(weight), (zturn[0], zturn[1]))
 
     def ring_send(src, dst, k):
-        for a, b in FAR:
+        for a, b in sorted(FAR, key=away):
             send(src, dst.at[FAR.index((-a, -b))], k, device(a, b))
 
-    q_own = overlaps(w, [])
+    q_own = overlaps(w)
     qbuf[...] = q_own
     ring_send(qbuf, qrecv, 3)
     for n, v in enumerate(split(jnp.concatenate([jnp.swapaxes(z, 0, 1) for z in zs], axis=0))):
@@ -572,7 +575,7 @@
 
     of_atoms = jnp.concatenate(
         [
-            jnp.sum(q * coef_h, axis=0, keepdims=True), jnp.sum(q * coef_s, axis=0, keepdims=True),
+            jnp.sum(q * coef_h[:5], axis=0, keepdims=True), jnp.sum(q * coef_s[:5], axis=0, keepdims=True),
         ],
         axis=0,
     )
@@ -581,7 +584,7 @@
     near = of_atoms * (rel_y == 0).astype(F32)
     esend[1] = near * (rel_x <= 0).astype(F32) + local + nrecv[0]
     esend[0] = near * (rel_x <= 1).astype(F32) + local + nrecv[0] + nrecv[1]
-    for n, (a, b) in enumerate(WINDOWS):
+    for n, (a, b) in sorted(enumerate(WINDOWS), key=lambda x: away(x[1])):
         send(esend.at[a // 6], ebuf.at[n], 4, device(-a, -b))
 
     both_terms = correction(jnp.concatenate([weights(coef_h), weights(coef_s)], axis=0))
@@ -592,17 +595,10 @@
 
     def share(first, second, mine, table, k):
         mine[...] = jnp.where(lane < 64, first, second)
-        table[me] = mine[...]
-
-        for a in range(nx):
-            for b in range(ny):
-                if (a, b) != (0, 0):
-                    send(mine, table.at[me], k, device(a, b))
-
-    def shared(table, k):
-        arrive(table.at[pl.ds(0, nx * ny - 1)], k)
-        total = jnp.sum(table[...], axis=0)
-        return total[:, 0:1], total[:, 64:65]
+
+        others = [(a, b) for a in range(nx) for b in range(ny) if (a, b) != (0, 0)]
+        for a, b in sorted(others, key=away):
+            send(mine, table.at[me], k, device(a, b))
 
     flat = from_right(jnp.concatenate([h_w, s_w], axis=1), "down_z")
     lower, upper = flat[:, 256:384], flat[:, 384:]
@@ -654,6 +650,8 @@
     residual = h_w - energy * s_w
     resid[...] = residual
     keep(1)
+    level[...] = lane * 0.0 + energy
+    keep(3)
     x1 = x1 - energy * pltpu.roll(x1, 64, 1)
     flat = from_right(x1, "up_zero_z")
     arrive(bhalo, 5)
@@ -670,7 +668,7 @@
     send(dirs.at[pl.ds(80, 48)], halo2.at[pl.ds(0, 48)], 8, device(1, 0))
     send(stage.at[pl.ds(48, 24)], halo2.at[pl.ds(120, 24)], 8, device(0, -1))
     send(stage.at[pl.ds(72, 24)], halo2.at[pl.ds(96, 24)], 8, device(0, 1))
-    q_own = overlaps(direction, [])
+    q_own = overlaps(direction)
     qbuf2[...] = q_own
     ring_send(qbuf2, qrecv2, 9)
     keep(0)
@@ -686,6 +684,7 @@
     share(along, square, lsend, lbuf, 10)
     changes[...] = change
     keep(2)
+    keep(4)
 
     left(infos.at[pl.ds(0, 8)], 0)
     left(halo, 1)
@@ -702,17 +701,17 @@
     left(qrecv2, 9)
     left(lbuf.at[pl.ds(0, nx * ny - 1)], 10)
 
-    along, square = shared(lbuf, 10)
-    sums_ref[...] = jnp.where(lane < 64, -along / square, energy)
-    for n in range(3):
+    arrive(lbuf.at[pl.ds(0, nx * ny - 1)], 10)
+    for n in range(5):
         kept(n).wait()
 
 
-def finish(w_ref, dirs_ref, resid_ref, change_ref, sums_ref, bands_ref, new_ref, energy_ref):
-    step = sums_ref[0:1, 0:1]
+def finish(w_ref, dirs_ref, resid_ref, change_ref, level_ref, sums_ref, bands_ref, new_ref, energy_ref):
+    sums = jnp.sum(sums_ref[...], axis=0)
+    step = -sums[:, 0:1] / sums[:, 64:65]
     bands_ref[...] = w_ref[...] + step * dirs_ref[...]
     new_ref[...] = resid_ref[...] + step * change_ref[...]
-    energy_ref[0] = sums_ref[0, 127]
+    energy_ref[0] = level_ref[0, 0]
 
 
 def solution(mesh):
@@ -726,11 +725,13 @@
         v = lambda *dims: pltpu.VMEM(dims, F32)
         hbm = pl.BlockSpec(memory_space=pltpu.HBM)
         grid = jax.ShapeDtypeStruct((128, 128), F32)
-        dirs, resid, changes, sums = pl.pallas_call(
+        parts = pl.pallas_call(
             functools.partial(kernel, shape, table),
-            out_shape=(grid, grid, grid, jax.ShapeDtypeStruct((1, 128), F32)),
+            out_shape=(
+                grid, grid, grid, jax.ShapeDtypeStruct((1, 128), F32), jax.ShapeDtypeStruct((nx * ny, 1, 128), F32),
+            ),
             in_specs=[hbm] * 7,
-            out_specs=(hbm, hbm, hbm, vmem),
+            out_specs=(hbm,) * 5,
             scratch_shapes=[
                 v(128, 128),
                 v(128, 32),
@@ -750,10 +751,10 @@
                 v(16, 8, 256),
                 v(2, 128, 128),
                 v(nb, 32, 128),
-                v(8, 128),
-                v(14, 8, 128),
-                v(8, 128),
-                v(14, 8, 128),
+                v(5, 128),
+                v(14, 5, 128),
+                v(5, 128),
+                v(14, 5, 128),
                 v(2, 128, 128),
                 v(2, 16, 128),
                 v(2, 48, 128),
@@ -766,14 +767,14 @@
                 v(2, 128),
                 v(2, 2, 128),
                 v(1, 128),
-                v(nx * ny, 1, 128),
+                v(1, 128),
                 pltpu.VMEM((2, 128, 512), BF16),
                 pltpu.VMEM((2, 512, 128), BF16),
                 v(5, 128, 128),
                 pltpu.SemaphoreType.DMA((7,)),
                 pltpu.SemaphoreType.DMA((13,)),
                 pltpu.SemaphoreType.DMA((13,)),
-                pltpu.SemaphoreType.DMA((3,)),
+                pltpu.SemaphoreType.DMA((5,)),
             ],
             compiler_params=pltpu.CompilerParams(
                 collective_id=0, has_side_effects=True, vmem_limit_bytes=60 << 20
@@ -790,10 +791,10 @@
         bands, resid, energy = pl.pallas_call(
             finish,
             out_shape=(grid, grid, jax.ShapeDtypeStruct((1,), F32)),
-            in_specs=[vmem] * 5,
+            in_specs=[vmem] * 4 + [smem, vmem],
             out_specs=(vmem, vmem, smem),
             compiler_params=pltpu.CompilerParams(vmem_limit_bytes=60 << 20),
-        )(wave_bands.reshape(128, 128), dirs, resid, changes, sums)
+        )(wave_bands.reshape(128, 128), *parts)
         return bands.reshape(1, CX, CY, NZ), resid.reshape(1, CX, CY, NZ), energy
 
     return jax.shard_map(

time: 38.8 us -> 37.9 us (0.977)
  Pallas kernels: 38 us -> 37.1 us
    pallas_call x1, Pallas kernels: 36.3 us -> 35.3 us  [on_device(): pl.pallas_call(functools.partial(kernel, shape, table), out_shape=(grid,...]
where the time goes in v4:
time: 37.9 us; the launch traced here: 37.7 us
  Pallas kernels  37.1 us (98%)
  between operations  0.64 us (2%)
    pallas_call x1, Pallas kernels, on_device(): pl.pallas_call(functools.partial(kernel, shape, table), out_shape=(grid,...  35.3 us
    pallas_call x1, Pallas kernels, on_device(): pl.pallas_call(finish, out_shape=(grid, grid, jax.ShapeDtypeStruct((1,),...  1.8 us

profile of v4, /device:TPU:1, one launch (start us, length us, event | category | flops | bytes accessed | tf_op | source)
XLA Modules:
  0.0 37.7 jit_solution(12116943362134351647)
XLA Ops:
  0.6 35.3 %shard_map.94 = (f32[128,128]{1,0:T(8,128)}, f32[128,128]{1,0:T(8,128)}, f32[128,128]{1,0:T(8,128)}, f32[1,128]{1,0:T(1,128)}, f32[64,1,128]{2,1,0:T(1,128)}) custom-call(f32[128,128]{1,0:T(8,128)} %bitcast.11, f32[128,32]{1,0:T(8,128)} %bitcast.13, s32[1,3,1,4]{3,2,1,0:T(1,128)} %bitcast.16, s32[1,1,4]{2,1,0:T(1,128)} %refs_3_.1, f32[9,4,9]{2,1,0:T(4,128)} %bitcast.14, ...), custom_call_target="tpu_custom_call" | custom-call | tf_op jit(solution)/shard_map/pallas_call | solution.py:728
  35.9 1.8 %shard_map.95 = (f32[128,128]{1,0:T(8,128)}, f32[128,128]{1,0:T(8,128)}, f32[1]{0:T(128)}) custom-call(f32[128,128]{1,0:T(8,128)} %bitcast.12, f32[128,128]{1,0:T(8,128)} %get-tuple-element.11.dirs_ref, f32[128,128]{1,0:T(8,128)} %get-tuple-element.12.resid_ref, f32[128,128]{1,0:T(8,128)} %get-tuple-element.13.change_ref, ...), custom_call_target="tpu_custom_call" | custom-call | tf_op jit(solution)/shard_map/pallas_call | solution.py:791

commit v5 on v4

--- a/solution.py
+++ b/solution.py
@@ -391,10 +391,10 @@
     row8 = lax.broadcasted_iota(jnp.int32, (8, 128), 0)
     loads[0].wait()
     loads[1].wait()
-    centres = jnp.zeros((8, 128), F32)
+    centres = jnp.zeros((1, 128), F32)
     for k in range(ATOMS):
         for m, v in enumerate((offs_ref[0, 0, 0, k], offs_ref[0, 1, 0, k], offs_ref[0, 2, 0, k], cnt_ref[0, 0, k])):
-            centres = jnp.where((lax.rem(row8, 4) == k) & (lane8 == m), v.astype(F32), centres)
+            centres = jnp.where(lane == 4 * m + k, v.astype(F32), centres)
     geo[...] = centres
     geos[slot] = centres
     loads[4].wait()
@@ -447,15 +447,17 @@
     kin = from_left("kin_own", w) + from_right(w, "kin_z")
 
     arrive(geos.at[pl.ds(0, 8)], 11)
-    centres = jnp.swapaxes(geos[...].reshape(128, 128), 0, 1)
+    chosen = ((lax.rem(lane8, 4) == lax.rem(row8, 4)) & (lane8 < 16)).astype(F32)
+    turned = jnp.swapaxes((geos[...] * chosen[None]).reshape(128, 128), 0, 1)
+    centres = [jnp.sum(turned[4 * m : 4 * m + 4], axis=0, keepdims=True) for m in range(4)]
     slot_x, slot_y = lane // 32, (lane // 8) % 4
     right_lane = (lane // 4) % 2 == 1
     rel_x = lax.rem(slot_x - ix + 1 + 16, 4) - 1
     rel_y = lax.rem(slot_y - iy + 1 + 16, 4) - 1
-    centre_x = centres[0:1, :] + (rel_x * CX).astype(F32)
-    centre_y = centres[1:2, :] + (rel_y * CY).astype(F32)
-    centre_z = centres[2:3, :]
-    count = centres[3:4, :]
+    centre_x = centres[0] + (rel_x * CX).astype(F32)
+    centre_y = centres[1] + (rel_y * CY).astype(F32)
+    centre_z = centres[2]
+    count = centres[3]
     active = (projector_of(row8, jnp.broadcast_to(right_lane, (8, 128))).astype(F32) < count).astype(F32)
 
     def bells(n, centre):
@@ -661,6 +663,9 @@
     ) + (GAIN[0] * SIDE[0]) * from_right(residual, "zero_z")
 
     dirs[...] = direction
+    q_own = overlaps(direction)
+    qbuf2[...] = q_own
+    ring_send(qbuf2, qrecv2, 9)
     for j in range(3):
         stage[48 + 8 * j : 56 + 8 * j, :] = dirs[pl.ds(j, 8, stride=16), :]
         stage[72 + 8 * j : 80 + 8 * j, :] = dirs[pl.ds(13 + j, 8, stride=16), :]
@@ -668,9 +673,6 @@
     send(dirs.at[pl.ds(80, 48)], halo2.at[pl.ds(0, 48)], 8, device(1, 0))
     send(stage.at[pl.ds(48, 24)], halo2.at[pl.ds(120, 24)], 8, device(0, -1))
     send(stage.at[pl.ds(72, 24)], halo2.at[pl.ds(96, 24)], 8, device(0, 1))
-    q_own = overlaps(direction)
-    qbuf2[...] = q_own
-    ring_send(qbuf2, qrecv2, 9)
     keep(0)
     change = from_left("kin_own", direction) + from_right(direction, "kin_z")
     change = change + (potential - energy) * direction
@@ -679,8 +681,10 @@
     arrive(qrecv2, 9)
     q = gather_overlaps(q_own, qrecv2)
     change = change + correction(weights(coefficients(q, 0) - energy * coefficients(q, 1)))
-    along = total_of(jnp.sum(residual * change, axis=0, keepdims=True))
-    square = total_of(jnp.sum(change * change, axis=0, keepdims=True))
+    along = jnp.sum(residual * change, axis=0, keepdims=True)
+    square = jnp.sum(change * change, axis=0, keepdims=True)
+    along = along + pltpu.roll(along, 64, 1)
+    square = square + pltpu.roll(square, 64, 1)
     share(along, square, lsend, lbuf, 10)
     changes[...] = change
     keep(2)
@@ -708,7 +712,10 @@
 
 def finish(w_ref, dirs_ref, resid_ref, change_ref, level_ref, sums_ref, bands_ref, new_ref, energy_ref):
     sums = jnp.sum(sums_ref[...], axis=0)
-    step = -sums[:, 0:1] / sums[:, 64:65]
+    first = lax.broadcasted_iota(jnp.int32, (1, 128), 1) < 64
+    along = jnp.sum(jnp.where(first, sums, 0.0), axis=1, keepdims=True)
+    square = jnp.sum(jnp.where(first, 0.0, sums), axis=1, keepdims=True)
+    step = -along / square
     bands_ref[...] = w_ref[...] + step * dirs_ref[...]
     new_ref[...] = resid_ref[...] + step * change_ref[...]
     energy_ref[0] = level_ref[0, 0]
@@ -745,8 +752,8 @@
                 v(128, 128),
                 v(128, 128),
                 v(128, 128),
-                v(8, 128),
-                v(16, 8, 128),
+                v(1, 128),
+                v(16, 1, 128),
                 v(8, 256),
                 v(16, 8, 256),
                 v(2, 128, 128),

time: 37.9 us -> 37.6 us (level)
  no operation moved by 1% of the time
where the time goes in v5:
time: 37.6 us; the launch traced here: 37.4 us
  Pallas kernels  36.8 us (98%)
  between operations  0.64 us (2%)
    pallas_call x1, Pallas kernels, on_device(): pl.pallas_call(functools.partial(kernel, shape, table), out_shape=(grid,...  35 us
    pallas_call x1, Pallas kernels, on_device(): pl.pallas_call(finish, out_shape=(grid, grid, jax.ShapeDtypeStruct((1,),...  1.77 us

profile of v5, /device:TPU:1, one launch (start us, length us, event | category | flops | bytes accessed | tf_op | source)
XLA Modules:
  0.0 37.4 jit_solution(10152095618770572780)
XLA Ops:
  0.6 35.0 %shard_map.94 = (f32[128,128]{1,0:T(8,128)}, f32[128,128]{1,0:T(8,128)}, f32[128,128]{1,0:T(8,128)}, f32[1,128]{1,0:T(1,128)}, f32[64,1,128]{2,1,0:T(1,128)}) custom-call(f32[128,128]{1,0:T(8,128)} %bitcast.11, f32[128,32]{1,0:T(8,128)} %bitcast.13, s32[1,3,1,4]{3,2,1,0:T(1,128)} %bitcast.16, s32[1,1,4]{2,1,0:T(1,128)} %refs_3_.1, f32[9,4,9]{2,1,0:T(4,128)} %bitcast.14, ...), custom_call_target="tpu_custom_call" | custom-call | tf_op jit(solution)/shard_map/pallas_call | solution.py:735
  35.6 1.8 %shard_map.95 = (f32[128,128]{1,0:T(8,128)}, f32[128,128]{1,0:T(8,128)}, f32[1]{0:T(128)}) custom-call(f32[128,128]{1,0:T(8,128)} %bitcast.12, f32[128,128]{1,0:T(8,128)} %get-tuple-element.11.dirs_ref, f32[128,128]{1,0:T(8,128)} %get-tuple-element.12.resid_ref, f32[128,128]{1,0:T(8,128)} %get-tuple-element.13.change_ref, ...), custom_call_target="tpu_custom_call" | custom-call | tf_op jit(solution)/shard_map/pallas_call | solution.py:798

commit v6 on v5

--- a/solution.py
+++ b/solution.py
@@ -335,8 +335,8 @@
             )
         )
     ]
-    for load in loads:
-        load.start()
+    for n in (0, 1, 4):
+        loads[n].start()
 
     def held(name):
         rows, cols, places = table[name]
@@ -386,6 +386,9 @@
         pl.semaphore_signal(barrier, inc=1, device_id=device(0, 0, i), device_id_type=MESH)
     for a, b in GREET:
         pl.semaphore_signal(barrier, inc=1, device_id=device(a, b), device_id_type=MESH)
+    for n in (5, 2, 3, 6):
+        loads[n].start()
+
     lane = lax.broadcasted_iota(jnp.int32, (1, 128), 1)
     lane8 = lax.broadcasted_iota(jnp.int32, (8, 128), 1)
     row8 = lax.broadcasted_iota(jnp.int32, (8, 128), 0)

time: 37.6 us -> 37.6 us (level)
  no operation moved by 1% of the time
where the time goes in v6:
time: 37.6 us; the launch traced here: 37.4 us
  Pallas kernels  36.8 us (98%)
  between operations  0.64 us (2%)
    pallas_call x1, Pallas kernels, on_device(): pl.pallas_call(functools.partial(kernel, shape, table), out_shape=(grid,...  35 us
    pallas_call x1, Pallas kernels, on_device(): pl.pallas_call(finish, out_shape=(grid, grid, jax.ShapeDtypeStruct((1,),...  1.77 us

profile of v6, /device:TPU:1, one launch (start us, length us, event | category | flops | bytes accessed | tf_op | source)
XLA Modules:
  0.0 37.4 jit_solution(16537036144072566270)
XLA Ops:
  0.6 35.0 %shard_map.94 = (f32[128,128]{1,0:T(8,128)}, f32[128,128]{1,0:T(8,128)}, f32[128,128]{1,0:T(8,128)}, f32[1,128]{1,0:T(1,128)}, f32[64,1,128]{2,1,0:T(1,128)}) custom-call(f32[128,128]{1,0:T(8,128)} %bitcast.11, f32[128,32]{1,0:T(8,128)} %bitcast.13, s32[1,3,1,4]{3,2,1,0:T(1,128)} %bitcast.16, s32[1,1,4]{2,1,0:T(1,128)} %refs_3_.1, f32[9,4,9]{2,1,0:T(4,128)} %bitcast.14, ...), custom_call_target="tpu_custom_call" | custom-call | tf_op jit(solution)/shard_map/pallas_call | solution.py:738
  35.6 1.8 %shard_map.95 = (f32[128,128]{1,0:T(8,128)}, f32[128,128]{1,0:T(8,128)}, f32[1]{0:T(128)}) custom-call(f32[128,128]{1,0:T(8,128)} %bitcast.12, f32[128,128]{1,0:T(8,128)} %get-tuple-element.11.dirs_ref, f32[128,128]{1,0:T(8,128)} %get-tuple-element.12.resid_ref, f32[128,128]{1,0:T(8,128)} %get-tuple-element.13.change_ref, ...), custom_call_target="tpu_custom_call" | custom-call | tf_op jit(solution)/shard_map/pallas_call | solution.py:801
